TPU v7x, 32 devices: a whole 2x2x4 slice. The times are simulated.
32 devices in a mesh: curve: 8 (over z, x), group: 4 (over y, core).
Axes of the slice: x: 2, y: 2, z: 4, core: 2. Of those that a mesh axis runs over, the one named last changes fastest.
Arguments:
- positions: float32 [4, 128, 3, 128], P('group', 'curve'), may hold values from 0 to 5.2, as said below
- velocities: float32 [4, 128, 3, 128], P('group', 'curve'), may hold values from -3 to 3
- masses: float32 [4, 128, 128], P('group', 'curve'), may hold values from 0.003 to 0.03
- counts: int32 [4, 128], P('group', 'curve'), may hold values from 64 to 128
- neighbours_first: int32 [4, 128, 6], P('group', 'curve'), may hold values from 0 to 23, as said below
- sends_first: int32 [4, 64], P('group', 'curve'), may hold values from 0 to 15, as said below
- new_slot: int32 [4, 128], P('group', 'curve'), may hold values from 0 to 63, as said below
- neighbours_second: int32 [4, 128, 6], P('group', 'curve'), may hold values from 0 to 23, as said below
- sends_second: int32 [4, 64], P('group', 'curve'), may hold values from 0 to 15, as said below
Outputs:
- positions_out: float32 [4, 128, 3, 128], P('group', 'curve')
- velocities_out: float32 [4, 128, 3, 128], P('group', 'curve')
- densities_out: float32 [4, 128, 128], P('group', 'curve')
Inputs may be any that keep to these rules, and one draw needn't show every extreme that they name: `positions`: the particles of blocks c * 16 to c * 16 + 15 of every group have first component in [0.6 c, 0.6 c + 1) and other components in [0, 1). `neighbours_first`: A block's list holds 6 distinct candidate numbers, never the block's own slot. `neighbours_second`: A block's list holds 6 distinct candidate numbers, never the block's own slot. `sends_first`: each of a device's two lists of 4 holds distinct slots. `sends_second`: each of a device's two lists of 4 holds distinct slots. For each curve segment, new_slot over all groups' blocks of that segment is a permutation; from one device at most 2 blocks go to any one other group, and in every segment some device sends exactly 2 to some other group.
All inputs are finite; a program needn't handle non-finite values.
Results may differ from a plain program's by a relative error of at most 0.0003.
Values sent between devices are 32-bit elements; how exact they have to be, the bound alone decides.
A program may use at most 64 MiB of HBM per device.

v0:
```python
import jax
import jax.numpy as jnp
from jax import lax
from jax.sharding import PartitionSpec as P

KERNEL_SCALE = 4.0
SMOOTHING = 0.5
SOFTENING = 0.0025
BACKGROUND = 0.5
TIME_STEP = 0.1


def with_halo(block, sides, width):
    for axis, dim in sides:
        count = lax.axis_size(axis)
        forward = [(i, i + 1) for i in range(count - 1)]
        forward.append((count - 1, 0))
        backward = [(target, source) for source, target in forward]
        low = lax.ppermute(
            lax.slice_in_dim(block, block.shape[dim] - width, None, axis=dim), axis, forward
        )
        high = lax.ppermute(lax.slice_in_dim(block, 0, width, axis=dim), axis, backward)
        block = jnp.concatenate([low, block, high], axis=dim)
    return block


def kernel_density(target_x, source_x, source_mass):
    offsets = [
        target_x[:, None, axis_id, :, None] - source_x[:, :, axis_id, None, :]
        for axis_id in range(3)
    ]
    square = offsets[0] * offsets[0] + offsets[1] * offsets[1] + offsets[2] * offsets[2]
    weight = jnp.exp(-KERNEL_SCALE * square)
    return BACKGROUND + jnp.sum(weight * source_mass[:, :, None, :], axis=(1, 3))


def kernel_force(target_x, target_v, target_rho, source_x, source_v, source_mass, source_rho):
    offsets = [
        target_x[:, None, axis_id, :, None] - source_x[:, :, axis_id, None, :]
        for axis_id in range(3)
    ]
    square = offsets[0] * offsets[0] + offsets[1] * offsets[1] + offsets[2] * offsets[2]
    approach = offsets[0] * (target_v[:, None, 0, :, None] - source_v[:, :, 0, None, :])
    approach = approach + offsets[1] * (target_v[:, None, 1, :, None] - source_v[:, :, 1, None, :])
    approach = approach + offsets[2] * (target_v[:, None, 2, :, None] - source_v[:, :, 2, None, :])
    weight = jnp.exp(-KERNEL_SCALE * square)
    closing = SMOOTHING * jnp.minimum(approach, 0.0) / (square + SOFTENING)
    mine = target_rho[:, None, :, None]
    theirs = source_rho[:, :, None, :]
    factor = source_mass[:, :, None, :] * (
        1.0 / mine + 1.0 / theirs - closing / (0.5 * (mine + theirs))
    )
    factor = factor * (2.0 * KERNEL_SCALE) * weight
    return jnp.stack(
        [jnp.sum(factor * offsets[axis_id], axis=(1, 3)) for axis_id in range(3)], axis=1
    )


def batched(function, arrays):
    shaped = tuple((item.reshape((item.shape[0] // 4, 4) + item.shape[1:]) for item in arrays))
    result = lax.map(lambda piece: function(*piece), shaped)
    return result.reshape((-1,) + result.shape[2:])


def send_positions(field, picks):
    outgoing = jnp.take(field, picks, axis=0)
    half = picks.shape[0] // 2
    arrived = with_halo(outgoing, (("curve", 0),), half)
    return jnp.concatenate([field, arrived[:half], arrived[3 * half :]], axis=0)


def send_returned(field, picks):
    outgoing = jnp.take(field, picks, axis=0)
    half = picks.shape[0] // 2
    arrived = with_halo(outgoing, (("curve", 0),), half)
    return jnp.concatenate([field, arrived[:half], arrived[3 * half :]], axis=0)


def sph_step(positions, velocities, mass_live, neighbours, picks):
    blocks = positions.shape[0]
    own = jnp.arange(blocks, dtype=jnp.int32)[:, None]
    index = jnp.concatenate([own, neighbours], axis=1)
    table = send_positions(jnp.concatenate([positions, mass_live[:, None, :]], axis=1), picks)
    table_x = table[:, 0:3]
    table_m = table[:, 3]
    source_x = jnp.take(table_x, index, axis=0)
    source_m = jnp.take(table_m, index, axis=0)
    density = batched(kernel_density, (positions, source_x, source_m))
    second = send_returned(jnp.concatenate([velocities, density[:, None, :]], axis=1), picks)
    table_v = second[:, 0:3]
    table_r = second[:, 3]
    source_v = jnp.take(table_v, index, axis=0)
    source_r = jnp.take(table_r, index, axis=0)
    accel = batched(
        kernel_force, (positions, velocities, density, source_x, source_v, source_m, source_r)
    )
    new_velocity = velocities + TIME_STEP * accel
    new_position = positions + TIME_STEP * new_velocity
    return (new_position, new_velocity, density)


def repartition(packed, new_slot):
    blocks = packed.shape[0]
    group_id = lax.axis_index("group")
    slots = jnp.arange(blocks, dtype=jnp.int32)
    everything, targets = (
        lax.all_gather(packed, "group", axis=0, tiled=True),
        lax.all_gather(new_slot, "group", axis=0, tiled=True),
    )
    wanted = group_id * blocks + slots
    hits = (targets[None, :] == wanted[:, None]).astype(jnp.int32)
    source = jnp.sum(hits * jnp.arange(targets.shape[0], dtype=jnp.int32)[None, :], axis=1)
    return jnp.take(everything, source, axis=0)


def body(
    positions,
    velocities,
    masses,
    counts,
    neighbours_first,
    sends_first,
    new_slot,
    neighbours_second,
    sends_second,
):
    positions = positions[0]
    velocities = velocities[0]
    masses = masses[0]
    counts = counts[0]
    particle_ids = jnp.arange(masses.shape[-1], dtype=jnp.int32)
    live = (particle_ids[None, :] < counts[:, None]).astype(jnp.float32)
    mass_live = masses * live
    first_x, first_v, first_rho = sph_step(
        positions, velocities, mass_live, neighbours_first[0], sends_first[0]
    )
    packed = jnp.concatenate([first_x, first_v, mass_live[:, None, :]], axis=1)
    moved = repartition(packed, new_slot[0])
    final_x, final_v, final_rho = sph_step(
        moved[:, 0:3], moved[:, 3:6], moved[:, 6], neighbours_second[0], sends_second[0]
    )
    return (final_x[None], final_v[None], final_rho[None])


def solution(mesh):
    in_specs = (
        P("group", "curve", None, None),
        P("group", "curve", None, None),
        P("group", "curve", None),
        P("group", "curve"),
        P("group", "curve", None),
        P("group", "curve"),
        P("group", "curve"),
        P("group", "curve", None),
        P("group", "curve"),
    )
    out_specs = (
        P("group", "curve", None, None),
        P("group", "curve", None, None),
        P("group", "curve", None),
    )
    return jax.shard_map(body, mesh=mesh, in_specs=in_specs, out_specs=out_specs, check_vma=False)
```

profile of v0, /device:TPU:0, one launch (start us, length us, event | category | flops | bytes accessed | tf_op | source)
XLA Modules:
  0.0 92.3 jit_solution(6341338332447597693)
XLA Ops:
  4.3 3.0 %collective-permute-start = (f32[4,4,128]{2,1,0:T(4,128)S(1)}, f32[4,4,128]{2,1,0:T(4,128)S(1)}, u32[]{:S(2)}, u32[]{:S(2)}) collective-permute-start(f32[4,4,128]{2,1,0:T(4,128)S(1)} %get-tuple-element.427), channel_id=1, source_target_pairs={{0,4},{4,8},{8,12},{12,16},{16,20},{20,24},{24,28},{28,0},{1,5},{5... | collective-permute-start | bytes 24584 | tf_op jit(solution)/shard_map/ppermute | solution.py:19
  7.3 3.1 %collective-permute-start.1 = (f32[4,4,128]{2,1,0:T(4,128)S(1)}, f32[4,4,128]{2,1,0:T(4,128)S(1)}, u32[]{:S(2)}, u32[]{:S(2)}) collective-permute-start(f32[4,4,128]{2,1,0:T(4,128)S(1)} %get-tuple-element.428), channel_id=1, source_target_pairs={{4,0},{8,4},{12,8},{16,12},{20,16},{24,20},{28,24},{0,28},{5,1},{9... | collective-permute-start | bytes 24584 | tf_op jit(solution)/shard_map/ppermute | solution.py:22
  11.7 5.1 %all-reduce = s32[64]{0:T(128)S(1)} all-reduce(s32[64]{0:T(128)S(1)} %bitcast_dynamic-update-slice_fusion.2), channel_id=2, replica_groups=mesh['curve'=8,'group'=4] {'group'}, use_global_device_ids=true, to_apply=%add | all-reduce | flops 64 | bytes 512
  19.2 4.6 %while.40 = (s32[]{:T(128)}, f32[4,4,128]{2,1,0:T(4,128)S(1)}, f32[4,4,3,128]{3,1,2,0:T(4,128)S(1)}, f32[4,4,7,3,128]{4,1,2,3,0:T(4,128)S(1)}, f32[4,4,7,128]{3,2,1,0:T(8,128)S(1)}, /*index=5*/s32[]{:T(128)}) while((s32[]{:T(128)}, f32[4,4,128]{2,1,0:T(4,128)S(1)}, f32[4,4,3,128]{3,1,2,0:T(4,128)S(1)}, f32[4,4,7,3,128]{4,1,2,3,0:T(4,128)S(1)}, ...), condition=%wide.region_3.7_spmd, body=%wide.region_1.6_spmd.sunk | while | flops 5046274 | bytes 381013 | solution.py:61
  19.3 1.0 %multiply_reduce_fusion.4 = f32[4,128]{1,0:T(4,128)S(1)} fusion(f32[4,7,128]{2,1,0:T(8,128)S(1)} %dynamic-slice_bitcast_fusion.33, f32[4,7,128]{2,1,0:T(8,128)S(1)} %copy.294, f32[4,128]{1,0:T(4,128)S(1)} %get-tuple-element.639, f32[4,7,128]{2,1,0:T(8,128)S(1)} %copy.295, f32[4,128]{1,0:T(4,128)S(1)} %get-tuple-element.641, ...), kind=kLoop, calls=%fused_computation.13.clone.1 | loop fusion | flops 5045760 | bytes 65536 | tf_op jit(solution)/shard_map/while/body/eval_jaxpr/reduce_sum | solution.py:34
  20.5 1.0 %multiply_reduce_fusion.4 = f32[4,128]{1,0:T(4,128)S(1)} fusion(f32[4,7,128]{2,1,0:T(8,128)S(1)} %dynamic-slice_bitcast_fusion.33, f32[4,7,128]{2,1,0:T(8,128)S(1)} %copy.294, f32[4,128]{1,0:T(4,128)S(1)} %get-tuple-element.639, f32[4,7,128]{2,1,0:T(8,128)S(1)} %copy.295, f32[4,128]{1,0:T(4,128)S(1)} %get-tuple-element.641, ...), kind=kLoop, calls=%fused_computation.13.clone.1 | loop fusion | flops 5045760 | bytes 65536 | tf_op jit(solution)/shard_map/while/body/eval_jaxpr/reduce_sum | solution.py:34
  24.6 4.7 %collective-permute-start.3 = (f32[4,4,128]{2,1,0:T(4,128)S(1)}, f32[4,4,128]{2,1,0:T(4,128)S(1)}, u32[]{:S(2)}, u32[]{:S(2)}) collective-permute-start(f32[4,4,128]{2,1,0:T(4,128)S(1)} %get-tuple-element.426), channel_id=1, source_target_pairs={{4,0},{8,4},{12,8},{16,12},{20,16},{24,20},{28,24},{0,28},{5,1},{9... | collective-permute-start | bytes 24584 | tf_op jit(solution)/shard_map/ppermute | solution.py:22
  29.5 1.4 %collective-permute-done.2 = f32[4,4,128]{2,1,0:T(4,128)S(1)} collective-permute-done((f32[4,4,128]{2,1,0:T(4,128)S(1)}, f32[4,4,128]{2,1,0:T(4,128)S(1)}, u32[]{:S(2)}, u32[]{:S(2)}) %collective-permute-start.2) | collective-permute-done | bytes 8224 | tf_op jit(solution)/shard_map/ppermute | solution.py:19
  32.6 14.7 %while.41 = (s32[]{:T(128)}, f32[4,4,3,128]{3,1,2,0:T(4,128)S(1)}, f32[4,4,7,128]{3,2,1,0:T(8,128)S(1)}, f32[4,4,128]{2,1,0:T(4,128)S(1)}, f32[4,4,7,128]{3,2,1,...) while((s32[]{:T(128)}, f32[4,4,3,128]{3,1,2,0:T(4,128)S(1)}, ...), condition=%wide.region_8.12_spmd, body=%wide.region_4.11_spmd.sunk | while | flops 16061954 | bytes 807041 | solution.py:61
  32.8 3.4 %fusion.48 = (f32[4,128]{1,0:T(4,128)S(1)}, f32[4,128]{1,0:T(4,128)S(1)}, f32[4,128]{1,0:T(4,128)S(1)}) fusion(f32[4,7,128]{2,1,0:T(8,128)S(1)} %copy.297, f32[4,128]{1,0:T(4,128)S(1)} %get-tuple-element.655, f32[4,7,128]{2,1,0:T(8,128)S(1)} %get-tuple-element.656, f32[4,128]{1,0:T(4,128)S(1)} %get-tuple-element.657, f32[4,7,128]{2,1,0:T(8,128)S(1)} %copy.298, ...), kind=kLoop, calls=%fused_computation.41.clone.1 | loop fusion | flops 16054784 | bytes 151552 | tf_op jit(solution)/shard_map/while/body/eval_jaxpr/reduce_sum | solution.py:55
  36.5 3.4 %fusion.48 = (f32[4,128]{1,0:T(4,128)S(1)}, f32[4,128]{1,0:T(4,128)S(1)}, f32[4,128]{1,0:T(4,128)S(1)}) fusion(f32[4,7,128]{2,1,0:T(8,128)S(1)} %copy.297, f32[4,128]{1,0:T(4,128)S(1)} %get-tuple-element.655, f32[4,7,128]{2,1,0:T(8,128)S(1)} %get-tuple-element.656, f32[4,128]{1,0:T(4,128)S(1)} %get-tuple-element.657, f32[4,7,128]{2,1,0:T(8,128)S(1)} %copy.298, ...), kind=kLoop, calls=%fused_computation.41.clone.1 | loop fusion | flops 16054784 | bytes 151552 | tf_op jit(solution)/shard_map/while/body/eval_jaxpr/reduce_sum | solution.py:55
  40.2 3.4 %fusion.48 = (f32[4,128]{1,0:T(4,128)S(1)}, f32[4,128]{1,0:T(4,128)S(1)}, f32[4,128]{1,0:T(4,128)S(1)}) fusion(f32[4,7,128]{2,1,0:T(8,128)S(1)} %copy.297, f32[4,128]{1,0:T(4,128)S(1)} %get-tuple-element.655, f32[4,7,128]{2,1,0:T(8,128)S(1)} %get-tuple-element.656, f32[4,128]{1,0:T(4,128)S(1)} %get-tuple-element.657, f32[4,7,128]{2,1,0:T(8,128)S(1)} %copy.298, ...), kind=kLoop, calls=%fused_computation.41.clone.1 | loop fusion | flops 16054784 | bytes 151552 | tf_op jit(solution)/shard_map/while/body/eval_jaxpr/reduce_sum | solution.py:55
  43.9 3.4 %fusion.48 = (f32[4,128]{1,0:T(4,128)S(1)}, f32[4,128]{1,0:T(4,128)S(1)}, f32[4,128]{1,0:T(4,128)S(1)}) fusion(f32[4,7,128]{2,1,0:T(8,128)S(1)} %copy.297, f32[4,128]{1,0:T(4,128)S(1)} %get-tuple-element.655, f32[4,7,128]{2,1,0:T(8,128)S(1)} %get-tuple-element.656, f32[4,128]{1,0:T(4,128)S(1)} %get-tuple-element.657, f32[4,7,128]{2,1,0:T(8,128)S(1)} %copy.298, ...), kind=kLoop, calls=%fused_computation.41.clone.1 | loop fusion | flops 16054784 | bytes 151552 | tf_op jit(solution)/shard_map/while/body/eval_jaxpr/reduce_sum | solution.py:55
  47.5 5.7 %all_gather.7 = f32[64,7,128]{2,0,1:T(8,128)S(1)} all-gather(f32[16,7,128]{2,0,1:T(8,128)S(1)} %copy.233), channel_id=1, replica_groups=mesh['curve'=8,'group'=4] {'group'}, dimensions={0}, use_global_device_ids=true | all-gather | bytes 286720 | tf_op jit(solution)/shard_map/all_gather | solution.py:107
  54.8 4.8 %collective-permute-start.5 = (f32[4,4,128]{2,1,0:T(4,128)S(1)}, f32[4,4,128]{2,1,0:T(4,128)S(1)}, u32[]{:S(2)}, u32[]{:S(2)}) collective-permute-start(f32[4,4,128]{2,1,0:T(4,128)S(1)} %get-tuple-element.424), channel_id=1, source_target_pairs={{4,0},{8,4},{12,8},{16,12},{20,16},{24,20},{28,24},{0,28},{5,1},{9... | collective-permute-start | bytes 24584 | tf_op jit(solution)/shard_map/ppermute | solution.py:22
  59.7 1.5 %collective-permute-done.4 = f32[4,4,128]{2,1,0:T(4,128)S(1)} collective-permute-done((f32[4,4,128]{2,1,0:T(4,128)S(1)}, f32[4,4,128]{2,1,0:T(4,128)S(1)}, u32[]{:S(2)}, u32[]{:S(2)}) %collective-permute-start.4) | collective-permute-done | bytes 8224 | tf_op jit(solution)/shard_map/ppermute | solution.py:19
  62.8 4.6 %while.42 = (s32[]{:T(128)}, f32[4,4,128]{2,1,0:T(4,128)S(1)}, f32[4,4,3,128]{3,1,2,0:T(4,128)S(1)}, f32[4,4,7,3,128]{4,1,2,3,0:T(4,128)S(1)}, f32[4,4,7,128]{3,2,1,0:T(8,128)S(1)}, /*index=5*/s32[]{:T(128)}) while((s32[]{:T(128)}, f32[4,4,128]{2,1,0:T(4,128)S(1)}, f32[4,4,3,128]{3,1,2,0:T(4,128)S(1)}, f32[4,4,7,3,128]{4,1,2,3,0:T(4,128)S(1)}, ...), condition=%wide.region_11.15_spmd, body=%wide.region_9.14_spmd.sunk | while | flops 5046274 | bytes 381013 | solution.py:61
  68.2 4.8 %collective-permute-start.7 = (f32[4,4,128]{2,1,0:T(4,128)S(1)}, f32[4,4,128]{2,1,0:T(4,128)S(1)}, u32[]{:S(2)}, u32[]{:S(2)}) collective-permute-start(f32[4,4,128]{2,1,0:T(4,128)S(1)} %get-tuple-element.422), channel_id=1, source_target_pairs={{4,0},{8,4},{12,8},{16,12},{20,16},{24,20},{28,24},{0,28},{5,1},{9... | collective-permute-start | bytes 24584 | tf_op jit(solution)/shard_map/ppermute | solution.py:22
  73.0 1.6 %collective-permute-done.6 = f32[4,4,128]{2,1,0:T(4,128)S(1)} collective-permute-done((f32[4,4,128]{2,1,0:T(4,128)S(1)}, f32[4,4,128]{2,1,0:T(4,128)S(1)}, u32[]{:S(2)}, u32[]{:S(2)}) %collective-permute-start.6) | collective-permute-done | bytes 8224 | tf_op jit(solution)/shard_map/ppermute | solution.py:19
  76.3 14.7 %while.43 = (s32[]{:T(128)}, f32[4,4,3,128]{3,1,2,0:T(4,128)S(1)}, f32[4,4,7,128]{3,2,1,0:T(8,128)S(1)}, f32[4,4,128]{2,1,0:T(4,128)S(1)}, f32[4,4,7,128]{3,2,1,...) while((s32[]{:T(128)}, f32[4,4,3,128]{3,1,2,0:T(4,128)S(1)}, ...), condition=%wide.region_16.20_spmd, body=%wide.region_12.19_spmd.sunk | while | flops 16061954 | bytes 807037 | solution.py:61
  76.5 3.4 %fusion.50 = (f32[4,128]{1,0:T(4,128)S(1)}, f32[4,128]{1,0:T(4,128)S(1)}, f32[4,128]{1,0:T(4,128)S(1)}) fusion(f32[4,7,128]{2,1,0:T(8,128)S(1)} %copy.306, f32[4,128]{1,0:T(4,128)S(1)} %get-tuple-element.697, f32[4,7,128]{2,1,0:T(8,128)S(1)} %get-tuple-element.698, f32[4,128]{1,0:T(4,128)S(1)} %get-tuple-element.699, f32[4,7,128]{2,1,0:T(8,128)S(1)} %copy.307, ...), kind=kLoop, calls=%fused_computation.101.clone.1 | loop fusion | flops 16054784 | bytes 151552 | tf_op jit(solution)/shard_map/while/body/eval_jaxpr/reduce_sum | solution.py:55
  80.2 3.4 %fusion.50 = (f32[4,128]{1,0:T(4,128)S(1)}, f32[4,128]{1,0:T(4,128)S(1)}, f32[4,128]{1,0:T(4,128)S(1)}) fusion(f32[4,7,128]{2,1,0:T(8,128)S(1)} %copy.306, f32[4,128]{1,0:T(4,128)S(1)} %get-tuple-element.697, f32[4,7,128]{2,1,0:T(8,128)S(1)} %get-tuple-element.698, f32[4,128]{1,0:T(4,128)S(1)} %get-tuple-element.699, f32[4,7,128]{2,1,0:T(8,128)S(1)} %copy.307, ...), kind=kLoop, calls=%fused_computation.101.clone.1 | loop fusion | flops 16054784 | bytes 151552 | tf_op jit(solution)/shard_map/while/body/eval_jaxpr/reduce_sum | solution.py:55
  83.9 3.4 %fusion.50 = (f32[4,128]{1,0:T(4,128)S(1)}, f32[4,128]{1,0:T(4,128)S(1)}, f32[4,128]{1,0:T(4,128)S(1)}) fusion(f32[4,7,128]{2,1,0:T(8,128)S(1)} %copy.306, f32[4,128]{1,0:T(4,128)S(1)} %get-tuple-element.697, f32[4,7,128]{2,1,0:T(8,128)S(1)} %get-tuple-element.698, f32[4,128]{1,0:T(4,128)S(1)} %get-tuple-element.699, f32[4,7,128]{2,1,0:T(8,128)S(1)} %copy.307, ...), kind=kLoop, calls=%fused_computation.101.clone.1 | loop fusion | flops 16054784 | bytes 151552 | tf_op jit(solution)/shard_map/while/body/eval_jaxpr/reduce_sum | solution.py:55
  87.5 3.4 %fusion.50 = (f32[4,128]{1,0:T(4,128)S(1)}, f32[4,128]{1,0:T(4,128)S(1)}, f32[4,128]{1,0:T(4,128)S(1)}) fusion(f32[4,7,128]{2,1,0:T(8,128)S(1)} %copy.306, f32[4,128]{1,0:T(4,128)S(1)} %get-tuple-element.697, f32[4,7,128]{2,1,0:T(8,128)S(1)} %get-tuple-element.698, f32[4,128]{1,0:T(4,128)S(1)} %get-tuple-element.699, f32[4,7,128]{2,1,0:T(8,128)S(1)} %copy.307, ...), kind=kLoop, calls=%fused_computation.101.clone.1 | loop fusion | flops 16054784 | bytes 151552 | tf_op jit(solution)/shard_map/while/body/eval_jaxpr/reduce_sum | solution.py:55
  (328 shorter events, 23.7 us)
Async XLA Ops:
  0.6 9.8 %copy-start.7 = (u32[32]{0:T(128)S(1)}, u32[32]{0:T(128)}, u32[]{:S(2)}) copy-start(u32[32]{0:T(128)} %constant.161) | copy-start | bytes 388
  0.6 16.8 %copy-start.2 = (f32[1,16,3,128]{3,1,2,0:T(8,128)S(1)}, f32[1,16,3,128]{3,1,2,0:T(8,128)}, u32[]{:S(2)}) copy-start(f32[1,16,3,128]{3,1,2,0:T(8,128)} %param.23) | copy-start | bytes 73732
  0.7 11.0 %copy-start.5 = (s32[1,16]{1,0:T(1,128)S(1)}, s32[1,16]{1,0:T(1,128)}, u32[]{:S(2)}) copy-start(s32[1,16]{1,0:T(1,128)} %param.29) | copy-start | bytes 196
  0.7 16.4 %copy-start.6 = (s32[1,8]{1,0:T(1,128)S(1)}, s32[1,8]{1,0:T(1,128)}, u32[]{:S(2)}) copy-start(s32[1,8]{1,0:T(1,128)} %param.31) | copy-start | bytes 100
  0.7 16.4 %copy-start.4 = (s32[1,16,6]{1,0,2:T(1,128)S(1)}, s32[1,16,6]{1,0,2:T(1,128)}, u32[]{:S(2)}) copy-start(s32[1,16,6]{1,0,2:T(1,128)} %param.27) | copy-start | bytes 1156
  0.7 16.4 %copy-start.3 = (s32[1,16,6]{1,0,2:T(1,128)S(1)}, s32[1,16,6]{1,0,2:T(1,128)}, u32[]{:S(2)}) copy-start(s32[1,16,6]{1,0,2:T(1,128)} %param.30) | copy-start | bytes 1156
  0.7 16.7 %copy-start = (f32[1,16,3,128]{3,1,2,0:T(8,128)S(1)}, f32[1,16,3,128]{3,1,2,0:T(8,128)}, u32[]{:S(2)}) copy-start(f32[1,16,3,128]{3,1,2,0:T(8,128)} %param.24) | copy-start | bytes 73732
  4.3 13.2 %collective-permute-start = (f32[4,4,128]{2,1,0:T(4,128)S(1)}, f32[4,4,128]{2,1,0:T(4,128)S(1)}, u32[]{:S(2)}, u32[]{:S(2)}) collective-permute-start(f32[4,4,128]{2,1,0:T(4,128)S(1)} %get-tuple-element.427), channel_id=1, source_target_pairs={{0,4},{4,8},{8,12},{12,16},{16,20},{20,24},{24,28},{28,0},{1,5},{5... | collective-permute-start | bytes 24584 | tf_op jit(solution)/shard_map/ppermute | solution.py:19
  7.3 10.2 %collective-permute-start.1 = (f32[4,4,128]{2,1,0:T(4,128)S(1)}, f32[4,4,128]{2,1,0:T(4,128)S(1)}, u32[]{:S(2)}, u32[]{:S(2)}) collective-permute-start(f32[4,4,128]{2,1,0:T(4,128)S(1)} %get-tuple-element.428), channel_id=1, source_target_pairs={{4,0},{8,4},{12,8},{16,12},{20,16},{24,20},{28,24},{0,28},{5,1},{9... | collective-permute-start | bytes 24584 | tf_op jit(solution)/shard_map/ppermute | solution.py:22
  24.5 6.4 %collective-permute-start.2 = (f32[4,4,128]{2,1,0:T(4,128)S(1)}, f32[4,4,128]{2,1,0:T(4,128)S(1)}, u32[]{:S(2)}, u32[]{:S(2)}) collective-permute-start(f32[4,4,128]{2,1,0:T(4,128)S(1)} %get-tuple-element.425), channel_id=1, source_target_pairs={{0,4},{4,8},{8,12},{12,16},{16,20},{20,24},{24,28},{28,0},{1,5},{5... | collective-permute-start | bytes 24584 | tf_op jit(solution)/shard_map/ppermute | solution.py:19
  24.6 6.3 %collective-permute-start.3 = (f32[4,4,128]{2,1,0:T(4,128)S(1)}, f32[4,4,128]{2,1,0:T(4,128)S(1)}, u32[]{:S(2)}, u32[]{:S(2)}) collective-permute-start(f32[4,4,128]{2,1,0:T(4,128)S(1)} %get-tuple-element.426), channel_id=1, source_target_pairs={{4,0},{8,4},{12,8},{16,12},{20,16},{24,20},{28,24},{0,28},{5,1},{9... | collective-permute-start | bytes 24584 | tf_op jit(solution)/shard_map/ppermute | solution.py:22
  54.7 6.4 %collective-permute-start.4 = (f32[4,4,128]{2,1,0:T(4,128)S(1)}, f32[4,4,128]{2,1,0:T(4,128)S(1)}, u32[]{:S(2)}, u32[]{:S(2)}) collective-permute-start(f32[4,4,128]{2,1,0:T(4,128)S(1)} %get-tuple-element.423), channel_id=1, source_target_pairs={{0,4},{4,8},{8,12},{12,16},{16,20},{20,24},{24,28},{28,0},{1,5},{5... | collective-permute-start | bytes 24584 | tf_op jit(solution)/shard_map/ppermute | solution.py:19
  54.8 6.3 %collective-permute-start.5 = (f32[4,4,128]{2,1,0:T(4,128)S(1)}, f32[4,4,128]{2,1,0:T(4,128)S(1)}, u32[]{:S(2)}, u32[]{:S(2)}) collective-permute-start(f32[4,4,128]{2,1,0:T(4,128)S(1)} %get-tuple-element.424), channel_id=1, source_target_pairs={{4,0},{8,4},{12,8},{16,12},{20,16},{24,20},{28,24},{0,28},{5,1},{9... | collective-permute-start | bytes 24584 | tf_op jit(solution)/shard_map/ppermute | solution.py:22
  68.1 6.5 %collective-permute-start.6 = (f32[4,4,128]{2,1,0:T(4,128)S(1)}, f32[4,4,128]{2,1,0:T(4,128)S(1)}, u32[]{:S(2)}, u32[]{:S(2)}) collective-permute-start(f32[4,4,128]{2,1,0:T(4,128)S(1)} %get-tuple-element.421), channel_id=1, source_target_pairs={{0,4},{4,8},{8,12},{12,16},{16,20},{20,24},{24,28},{28,0},{1,5},{5... | collective-permute-start | bytes 24584 | tf_op jit(solution)/shard_map/ppermute | solution.py:19
  68.2 6.4 %collective-permute-start.7 = (f32[4,4,128]{2,1,0:T(4,128)S(1)}, f32[4,4,128]{2,1,0:T(4,128)S(1)}, u32[]{:S(2)}, u32[]{:S(2)}) collective-permute-start(f32[4,4,128]{2,1,0:T(4,128)S(1)} %get-tuple-element.422), channel_id=1, source_target_pairs={{4,0},{8,4},{12,8},{16,12},{20,16},{24,20},{28,24},{0,28},{5,1},{9... | collective-permute-start | bytes 24584 | tf_op jit(solution)/shard_map/ppermute | solution.py:22
  91.0 1.3 %copy-start.1 = (f32[4,4,128]{2,1,0:T(4,128)}, f32[4,4,128]{2,1,0:T(4,128)S(1)}, u32[]{:S(2)}) copy-start(f32[4,4,128]{2,1,0:T(4,128)S(1)} %get-tuple-element.820) | copy-start | bytes 24580
where the time goes:
time: 92.6 us; the launch traced here: 92.3 us
  other arithmetic  39.6 us (43%)
  starting transfers between devices  20.6 us (22%)
  local copies, waits for them, and re-layouts  13.1 us (14%)
  blocking collectives  10.8 us (12%)
  waiting for transfers between devices  4.47 us (5%)
  between operations  1.93 us (2%)
  loops' own time  1.78 us (2%)
    reduce_sum x8, other arithmetic, kernel_force(): jnp.sum(factor * offsets[axis_id], axis=(1, 3))  27.3 us
    ppermute x4, starting transfers between devices, with_halo(): lax.ppermute(lax.slice_in_dim(block, 0, width, axis=dim), axis, backward)  17.4 us
    reduce_sum x8, other arithmetic, kernel_density(): jnp.sum(weight * source_mass[:, :, None, :], axis=(1, 3))  8.08 us
    all_gather x1, blocking collectives, repartition(): lax.all_gather(packed, 'group', axis=0, tiled=True)  5.7 us
    unnamed x1, blocking collectives  5.06 us
    ppermute x4, waiting for transfers between devices, with_halo(): lax.ppermute(lax.slice_in_dim(block, block.shape[dim] - width, None, axis...  4.46 us
    ppermute x4, starting transfers between devices, with_halo(): lax.ppermute(lax.slice_in_dim(block, block.shape[dim] - width, None, axis...  3.17 us
    unnamed x24, local copies, waits for them, and re-layouts  2.72 us
  transfers between devices with their start and end apart: 8, of which 3 were waited for; matrix products, arithmetic and copies ran while one was open for 2% of the time, Pallas kernels for 0%

commit v1 on v0

v1 whole, which is shorter than its diff:
```python
import functools
import math

import jax
import jax.numpy as jnp
from jax import lax
from jax.experimental import pallas as pl
from jax.experimental.pallas import tpu as pltpu
from jax.sharding import PartitionSpec as P

KERNEL_SCALE = 4.0
SOFTENING = 0.0025
BACKGROUND = 0.5
TIME_STEP = 0.1
SPACING = 0.6
MOVE_CAP = 2
LOG2E = math.log2(math.e)
SCALE = -KERNEL_SCALE * LOG2E
DEAD = -200.0
MESH = pl.DeviceIdType.MESH
F32 = jnp.float32
BF16 = jnp.bfloat16


def split(value):
    high = value.astype(BF16).astype(F32)
    rest = value - high
    middle = rest.astype(BF16).astype(F32)
    return high, middle, rest - middle


def source_rows(value):
    high, middle, low = split(value)
    return [high, middle, low, high, high, middle]


def target_rows(value):
    high, middle, low = split(value)
    return [high, high, high, middle, low, middle]


def rows_of(shape):
    return lax.broadcasted_iota(jnp.int32, shape, 0)


def moments(state, corner):
    row = rows_of(state.shape)
    state = state - jnp.where(row == 0, corner + 0.5, jnp.where(row < 3, 0.5, 0.0))
    square = jnp.sum(jnp.where(row < 3, state * state, 0.0), axis=0, keepdims=True)
    after = pltpu.roll(state, 3, 0)
    cross = jnp.sum(
        jnp.where((row >= 3) & (row < 6), state * after, 0.0), axis=0, keepdims=True
    )
    return row, state, after, square, cross


def prepare_source(state, corner, source_t, source_m):
    row, state, after, square, cross = moments(state, corner)
    mass = state[6:7]
    logm = jnp.where(mass > 0.0, jnp.log(jnp.maximum(mass, 1e-30)) * LOG2E, DEAD)
    lower = jnp.where(row < 6, state, jnp.where(row == 6, 1.0, square))
    upper = jnp.where(row == 0, cross, jnp.where(row == 1, logm, 0.0))
    feature = jnp.concatenate([lower, upper], axis=0)
    width = state.shape[1]
    pieces = source_rows(feature)
    used = len(pieces) * feature.shape[0]
    pieces.append(jnp.zeros((width - used, width), F32))
    source_t[...] = jnp.concatenate(pieces, axis=0).T.astype(BF16)
    weighted = jnp.where(row < 7, lower * mass, 0.0)
    source_m[...] = jnp.concatenate(
        list(split(weighted)) + [jnp.zeros_like(weighted)], axis=0
    ).astype(BF16)


def prepare_target(state, corner, target_d, target_f):
    row, state, after, square, cross = moments(state, corner)
    width = state.shape[1]
    ahead = pltpu.roll(state, state.shape[0] - 3, 0)
    near = jnp.where(row < 3, (-2.0 * SCALE) * state, 0.0)
    tail = jnp.where(row == 7, SCALE, 0.0)
    plain = jnp.where(row == 6, SCALE * square, near + tail)
    soft = jnp.where(row == 6, SCALE * (square + SOFTENING), near + tail)
    closing = jnp.where(
        row < 3,
        -SCALE * ahead,
        jnp.where(row < 6, -SCALE * after, jnp.where(row == 6, SCALE * cross, 0.0)),
    )
    upper_d = jnp.where(row == 1, 1.0, 0.0)
    upper_c = jnp.where(row == 0, SCALE, 0.0)

    def table(lower, upper):
        pieces = target_rows(jnp.concatenate([lower, upper], axis=0))
        used = len(pieces) * 2 * lower.shape[0]
        pieces.append(jnp.zeros((width - used, width), F32))
        return jnp.concatenate(pieces, axis=0).astype(BF16)

    target_d[...] = table(plain, upper_d)
    target_f[:, 0:width] = table(soft, jnp.zeros_like(upper_c))
    target_f[:, width : 2 * width] = table(closing, upper_c)


def density_of(block, nbr, source_t, target_d):
    count = nbr.shape[0]
    target = target_d[block]
    total = None
    for item in range(count + 1):
        pick = block if item == 0 else nbr[item - 1, 0, block]
        power = jnp.dot(source_t[pick], target, preferred_element_type=F32)
        weight = jnp.exp2(power)
        total = weight if total is None else total + weight
    return BACKGROUND + jnp.sum(total, axis=0, keepdims=True)


def force_of(block, nbr, state, corner, rho, rho_col, inv_col, source_t, source_m, target_f):
    count = nbr.shape[0]
    width = state.shape[1]
    target = target_f[block]
    inverse = 1.0 / rho
    total = None
    for item in range(count + 1):
        pick = block if item == 0 else nbr[item - 1, 0, block]
        both = jnp.dot(source_t[pick], target, preferred_element_type=F32)
        soft = both[:, 0:width]
        closing = jnp.maximum(both[:, width : 2 * width], 0.0)
        bottom = soft * (rho_col[pick] + rho)
        viscous = closing * pl.reciprocal(bottom, approx=True)
        factor = jnp.exp2(soft) * (inv_col[pick] + inverse - viscous)
        part = jnp.dot(source_m[pick], factor.astype(BF16), preferred_element_type=F32)
        total = part if total is None else total + part
    rows = state.shape[0]
    sums = total[0:rows] + total[rows : 2 * rows] + total[2 * rows : 3 * rows]
    row = rows_of(state.shape)
    centred = state - jnp.where(row == 0, corner + 0.5, jnp.where(row < 3, 0.5, 0.0))
    strength = 2.0 * KERNEL_SCALE * math.exp(KERNEL_SCALE * SOFTENING)
    accel = strength * (centred * sums[6:7] - sums)
    velocity = state + TIME_STEP * pltpu.roll(accel, 3, 0)
    position = state + TIME_STEP * pltpu.roll(velocity, rows - 3, 0)
    return jnp.where(row < 3, position, jnp.where(row < 6, velocity, state))


def columns(rho, rho_col, inv_col):
    width = rho.shape[1]
    col = jnp.broadcast_to(rho, (width, width)).T
    rho_col[...] = col
    inv_col[...] = 1.0 / col


def kernel(
    n_curve, n_group,
    pos, vel, mass, counts, nbr1, sends1, slots_s, slots_v, nbr2, sends2,
    pos_out, vel_out, rho_out,
    table1, table2, land1, land2, kept, moved, out1, out2, out_m, rho1, rho2, rho_s1, rho_s2,
    source_t, source_m, target_d, target_f, rho_col, inv_col,
    slots_own, slots_in, code_v, code_s,
    send_sem, recv_sem, send_g, recv_g, code_sem,
):
    blocks = pos.shape[2]
    width = pos.shape[3]
    halo = sends1.shape[1] // 2
    mine = lax.axis_index("curve")
    group = lax.axis_index("group")
    lower = lax.rem(mine + n_curve - 1, n_curve)
    upper = lax.rem(mine + 1, n_curve)
    corner = SPACING * mine.astype(F32)
    barrier = pltpu.get_barrier_semaphore()
    for other in (lower, upper):
        pl.semaphore_signal(barrier, inc=1, device_id={"curve": other}, device_id_type=MESH)
    peers = [lax.rem(group + step, n_group) for step in range(1, n_group)]
    for other in peers:
        pl.semaphore_signal(barrier, inc=1, device_id={"group": other}, device_id_type=MESH)

    lane = lax.broadcasted_iota(jnp.int32, (1, width), 1)

    def load_state(block, carry):
        for axis in range(3):
            table1[block, axis : axis + 1, :] = pos[0, axis, pl.ds(block, 1), :]
            table1[block, 3 + axis : 4 + axis, :] = vel[0, axis, pl.ds(block, 1), :]
        live = jnp.where(lane < counts[0, block], mass[0, pl.ds(block, 1), :], 0.0)
        table1[block, 6:7, :] = live
        table1[block, 7:8, :] = jnp.zeros_like(live)
        return carry

    lax.fori_loop(0, blocks, load_state, 0, unroll=True)
    slots_own[...] = jnp.full(slots_own.shape, -1, jnp.int32)
    slots_own[:, 0:blocks] = slots_v[...]
    for item in range(2 * halo):
        out1[item] = table1[sends1[0, item]]
    pl.semaphore_wait(barrier, 2 + n_group - 1)

    def exchange(outgoing, landing, start, base):
        copies = []
        for side, other in ((0, lower), (1, upper)):
            copies.append(
                pltpu.make_async_remote_copy(
                    src_ref=outgoing.at[pl.ds(side * halo, halo)],
                    dst_ref=landing.at[pl.ds(start + (1 - side) * halo, halo)],
                    send_sem=send_sem.at[base + side],
                    recv_sem=recv_sem.at[base + side],
                    device_id={"curve": other},
                    device_id_type=MESH,
                )
            )
        for copy in copies:
            copy.start()
        return copies

    def finish(copies):
        for copy in copies:
            copy.wait()

    first = exchange(out1, land1, 0, 0)
    lists = []
    for step, other in enumerate(peers):
        copy = pltpu.make_async_remote_copy(
            src_ref=slots_own,
            dst_ref=slots_in.at[step],
            send_sem=send_g.at[step],
            recv_sem=recv_g.at[step],
            device_id={"group": other},
            device_id_type=MESH,
        )
        copy.start()
        lists.append(copy)

    def prepare_own(table):
        def run(block, carry):
            state = table[block]
            prepare_source(state, corner, source_t.at[block], source_m.at[block])
            prepare_target(state, corner, target_d.at[block], target_f.at[block])
            return carry

        lax.fori_loop(0, blocks, run, 0)

    def prepare_halo(land):
        def run(item, carry):
            block = blocks + item
            prepare_source(land[item], corner, source_t.at[block], source_m.at[block])
            return carry

        lax.fori_loop(0, 2 * halo, run, 0)

    def sph(table, land, nbr, sends, rho, rho_send, base, write):
        prepare_halo(land)

        def listed(item, carry):
            rho_send[item] = density_of(sends[0, item], nbr, source_t, target_d)
            return carry

        lax.fori_loop(0, 2 * halo, listed, 0)
        copies = exchange(rho_send, rho, blocks, base)

        def own(block, carry):
            value = density_of(block, nbr, source_t, target_d)
            rho[block] = value
            columns(value, rho_col.at[block], inv_col.at[block])
            return carry

        lax.fori_loop(0, blocks, own, 0)
        finish(copies)

        def halos(block, carry):
            columns(rho[block], rho_col.at[block], inv_col.at[block])
            return carry

        lax.fori_loop(blocks, blocks + 2 * halo, halos, 0)

        def push(block, carry):
            write(
                block,
                force_of(
                    block, nbr, table[block], corner, rho[block],
                    rho_col, inv_col, source_t, source_m, target_f,
                ),
            )
            return carry

        lax.fori_loop(0, blocks, push, 0)

    prepare_own(table1)
    finish(lists)
    wanted = rows_of((blocks, width)) + group * blocks
    lanes = lax.broadcasted_iota(jnp.int32, (blocks, width), 1)
    code = jnp.sum(jnp.where(slots_own[...] == wanted, lanes, 0), axis=1, keepdims=True)
    for step in range(n_group - 1):
        arrived = slots_in[step]
        here = (arrived >= group * blocks) & (arrived < (group + 1) * blocks)
        lead = jnp.min(jnp.where(here, lane, width), axis=1, keepdims=True)
        place = blocks + MOVE_CAP * step + jnp.where(lane > lead, 1, 0)
        code = code + jnp.sum(jnp.where(arrived == wanted, place, 0), axis=1, keepdims=True)
    code = jnp.minimum(code, moved.shape[0] - 1)
    code_v[...] = jnp.broadcast_to(code, code_v.shape)
    code_copy = pltpu.make_async_copy(code_v, code_s, code_sem)
    code_copy.start()
    finish(first)

    def keep(block, state):
        kept[block] = state

    sph(table1, land1, nbr1, sends1, rho1, rho_s1, 2, keep)

    moves = []
    for step, other in enumerate(peers):
        one = jnp.int32(0)
        two = jnp.int32(0)
        for block in reversed(range(blocks)):
            target = slots_s[0, block]
            goes = (target >= other * blocks) & (target < (other + 1) * blocks)
            two = jnp.where(goes, one, two)
            one = jnp.where(goes, block, one)
        out_m[step, 0] = kept[one]
        out_m[step, 1] = kept[two]
        copy = pltpu.make_async_remote_copy(
            src_ref=out_m.at[step],
            dst_ref=moved.at[pl.ds(blocks + MOVE_CAP * step, MOVE_CAP)],
            send_sem=send_g.at[n_group - 1 + step],
            recv_sem=recv_g.at[n_group - 1 + step],
            device_id={"group": other},
            device_id_type=MESH,
        )
        copy.start()
        moves.append(copy)
    code_copy.wait()
    for block in range(blocks):
        moved[block] = kept[block]
    finish(moves)
    for item in range(2 * halo):
        out2[item] = moved[code_s[sends2[0, item], 0]]
    second = exchange(out2, land2, 0, 4)
    for block in range(blocks):
        table2[block] = moved[code_s[block, 0]]
    prepare_own(table2)
    finish(second)

    def emit(block, state):
        for axis in range(3):
            pos_out[0, axis, pl.ds(block, 1), :] = state[axis : axis + 1]
            vel_out[0, axis, pl.ds(block, 1), :] = state[3 + axis : 4 + axis]
        rho_out[0, pl.ds(block, 1), :] = rho2[block]

    sph(table2, land2, nbr2, sends2, rho2, rho_s2, 6, emit)


def body(
    n_curve, n_group,
    positions, velocities, masses, counts, neighbours_first, sends_first, new_slot,
    neighbours_second, sends_second,
):
    blocks, width = masses.shape[1], masses.shape[2]
    halo = sends_first.shape[1] // 2
    whole = blocks + 2 * halo
    peers = n_group - 1
    vmem = pl.BlockSpec(memory_space=pltpu.VMEM)
    smem = pl.BlockSpec(memory_space=pltpu.SMEM)
    scratch = [
        pltpu.VMEM((blocks, 8, width), F32),
        pltpu.VMEM((blocks, 8, width), F32),
        pltpu.VMEM((2 * halo, 8, width), F32),
        pltpu.VMEM((2 * halo, 8, width), F32),
        pltpu.VMEM((blocks, 8, width), F32),
        pltpu.VMEM((blocks + MOVE_CAP * peers, 8, width), F32),
        pltpu.VMEM((2 * halo, 8, width), F32),
        pltpu.VMEM((2 * halo, 8, width), F32),
        pltpu.VMEM((peers, MOVE_CAP, 8, width), F32),
        pltpu.VMEM((whole, 1, width), F32),
        pltpu.VMEM((whole, 1, width), F32),
        pltpu.VMEM((2 * halo, 1, width), F32),
        pltpu.VMEM((2 * halo, 1, width), F32),
        pltpu.VMEM((whole, width, width), BF16),
        pltpu.VMEM((whole, 32, width), BF16),
        pltpu.VMEM((blocks, width, width), BF16),
        pltpu.VMEM((blocks, width, 2 * width), BF16),
        pltpu.VMEM((whole, width, width), F32),
        pltpu.VMEM((whole, width, width), F32),
        pltpu.VMEM((1, width), jnp.int32),
        pltpu.VMEM((peers, 1, width), jnp.int32),
        pltpu.VMEM((blocks, width), jnp.int32),
        pltpu.SMEM((blocks, width), jnp.int32),
        pltpu.SemaphoreType.DMA((8,)),
        pltpu.SemaphoreType.DMA((8,)),
        pltpu.SemaphoreType.DMA((2 * peers,)),
        pltpu.SemaphoreType.DMA((2 * peers,)),
        pltpu.SemaphoreType.DMA,
    ]
    turned = jax.ShapeDtypeStruct((1, 3, blocks, width), F32)
    positions_out, velocities_out, densities_out = pl.pallas_call(
        functools.partial(kernel, n_curve, n_group),
        out_shape=(
            turned,
            turned,
            jax.ShapeDtypeStruct(masses.shape, F32),
        ),
        in_specs=[vmem, vmem, vmem, smem, smem, smem, smem, vmem, smem, smem],
        out_specs=(vmem, vmem, vmem),
        scratch_shapes=scratch,
        compiler_params=pltpu.CompilerParams(
            collective_id=0, has_side_effects=True, vmem_limit_bytes=32 * 1024 * 1024
        ),
        name="sph",
    )(
        positions.transpose(0, 2, 1, 3), velocities.transpose(0, 2, 1, 3), masses, counts,
        neighbours_first.transpose(2, 0, 1), sends_first, new_slot,
        new_slot, neighbours_second.transpose(2, 0, 1), sends_second,
    )
    return (
        positions_out.transpose(0, 2, 1, 3), velocities_out.transpose(0, 2, 1, 3), densities_out,
    )


def solution(mesh):
    blocks4 = P("group", "curve", None, None)
    blocks3 = P("group", "curve", None)
    blocks2 = P("group", "curve")
    in_specs = (
        blocks4, blocks4, blocks3, blocks2, blocks3, blocks2, blocks2, blocks3, blocks2,
    )
    return jax.shard_map(
        functools.partial(body, mesh.shape["curve"], mesh.shape["group"]),
        mesh=mesh, in_specs=in_specs, out_specs=(blocks4, blocks4, blocks3), check_vma=False,
    )
```

time: 92.6 us -> 81.3 us (0.88)
  Pallas kernels: 0 us -> 75 us
  other arithmetic: 39.6 us -> 0 us
  starting transfers between devices: 20.6 us -> 0 us
  blocking collectives: 10.8 us -> 0 us
  local copies, waits for them, and re-layouts: 13.1 us -> 5.32 us
  waiting for transfers between devices: 4.47 us -> 0 us
  loops' own time: 1.78 us -> 0 us
  between operations: 1.93 us -> 0.69 us
    pallas_call x0 -> x1, Pallas kernels: none -> 75 us  [body(): pl.pallas_call(functools.partial(kernel, n_curve, n_group), out_shape=(tu...]
    reduce_sum x17 -> x0, other arithmetic: 35.6 us -> none  [the longest x8 27.3 us: kernel_force(): jnp.sum(factor * offsets[axis_id], axis=(1, 3))]
    ppermute x8 -> x0, starting transfers between devices: 20.6 us -> none  [the longest x4 17.4 us: with_halo(): lax.ppermute(lax.slice_in_dim(block, 0, width, axis=dim), axis, backward)]
    gather x17 -> x0, local copies, waits for them, and re-layouts: 8.35 us -> none  [the longest x2 1.46 us: sph_step(): source_v = jnp.take(table_v, index, axis=0)]
    all_gather x1 -> x0, blocking collectives: 5.7 us -> none  [repartition(): lax.all_gather(packed, 'group', axis=0, tiled=True)]
    unnamed x1 -> x0, blocking collectives: 5.06 us -> none
    ppermute x8 -> x0, waiting for transfers between devices: 4.47 us -> none  [the longest x4 4.46 us: with_halo(): lax.ppermute(lax.slice_in_dim(block, block.shape[dim] - width, None, axis...]
    unnamed x24 -> x21, local copies, waits for them, and re-layouts: 2.72 us -> 5.32 us
  transfers between devices with their start and end apart: 8 -> 0, of which waited for: 3 -> 0; matrix products, arithmetic and copies ran while one was open for 2% -> 0% of each run, Pallas kernels for 0% -> 0%
where the time goes in v1:
time: 81.3 us; the launch traced here: 81 us
  Pallas kernels  75 us (92%)
  local copies, waits for them, and re-layouts  5.32 us (7%)
    pallas_call x1, Pallas kernels, body(): pl.pallas_call(functools.partial(kernel, n_curve, n_group), out_shape=(tu...  75 us
    unnamed x21, local copies, waits for them, and re-layouts  5.32 us

profile of v1, /device:TPU:0, one launch (start us, length us, event | category | flops | bytes accessed | tf_op | source)
XLA Modules:
  0.0 81.0 jit_solution(9259359956845476936)
XLA Ops:
  0.6 0.0 copy-start.4
  0.6 0.0 copy-start.3
  0.7 0.0 copy-start.5
  0.7 0.0 copy-start.6
  0.7 0.0 copy-start.7
  0.7 0.6 copy-done.4
  1.3 0.0 copy-done.3
  1.3 0.0 copy-done.5
  1.3 0.0 copy-done.6
  1.3 0.0 copy-done.7
  1.4 0.0 copy-start
  1.4 0.7 copy-done
  2.1 0.0 copy-start.1
  2.1 0.7 copy-done.1
  2.8 0.0 copy-start.2
  2.8 0.7 copy-done.2
  3.5 0.0 copy-start.8
  3.5 0.7 copy-done.8
  4.2 75.0 %sph.1 = (f32[1,3,16,128]{3,2,1,0:T(8,128)S(1)}, f32[1,3,16,128]{3,2,1,0:T(8,128)S(1)}, f32[1,16,128]{2,1,0:T(8,128)S(1)}) custom-call(f32[1,3,16,128]{3,2,1,0:T(8,128)S(1)} %bitcast.6, f32[1,3,16,128]{3,2,1,0:T(8,128)S(1)} %bitcast.7, f32[1,16,128]{2,1,0:T(8,128)S(1)} %copy-done.2, s32[1,16]{1,0:T(1,128)S(1)} %copy-done.6, s32[6,1,16]{2,1,0:T(1,128)S(1)} %bitcast.10, ...), custom_call_target="tpu_custom_call" | custom-call | tf_op jit(solution)/shard_map/sph/pallas_call | solution.py:385
  79.2 0.6 copy.15
  79.8 0.6 copy.16
  80.4 0.6 copy.17
Async XLA Ops:
  0.6 0.7 copy-start.4
  0.6 0.7 copy-start.3
  0.7 0.7 copy-start.5
  0.7 0.7 copy-start.6
  0.7 0.7 copy-start.7
  1.4 0.7 copy-start
  2.1 0.7 copy-start.1
  2.8 0.7 copy-start.2
  3.5 0.7 copy-start.8

commit v2 on v1

--- a/solution.py
+++ b/solution.py
@@ -229,7 +229,7 @@
             prepare_target(state, corner, target_d.at[block], target_f.at[block])
             return carry
 
-        lax.fori_loop(0, blocks, run, 0)
+        lax.fori_loop(0, blocks, run, 0, unroll=8)
 
     def prepare_halo(land):
         def run(item, carry):
@@ -237,7 +237,7 @@
             prepare_source(land[item], corner, source_t.at[block], source_m.at[block])
             return carry
 
-        lax.fori_loop(0, 2 * halo, run, 0)
+        lax.fori_loop(0, 2 * halo, run, 0, unroll=8)
 
     def sph(table, land, nbr, sends, rho, rho_send, base, write):
         prepare_halo(land)
@@ -246,7 +246,7 @@
             rho_send[item] = density_of(sends[0, item], nbr, source_t, target_d)
             return carry
 
-        lax.fori_loop(0, 2 * halo, listed, 0)
+        lax.fori_loop(0, 2 * halo, listed, 0, unroll=4)
         copies = exchange(rho_send, rho, blocks, base)
 
         def own(block, carry):
@@ -255,14 +255,14 @@
             columns(value, rho_col.at[block], inv_col.at[block])
             return carry
 
-        lax.fori_loop(0, blocks, own, 0)
+        lax.fori_loop(0, blocks, own, 0, unroll=4)
         finish(copies)
 
         def halos(block, carry):
             columns(rho[block], rho_col.at[block], inv_col.at[block])
             return carry
 
-        lax.fori_loop(blocks, blocks + 2 * halo, halos, 0)
+        lax.fori_loop(blocks, blocks + 2 * halo, halos, 0, unroll=8)
 
         def push(block, carry):
             write(
@@ -274,7 +274,7 @@
             )
             return carry
 
-        lax.fori_loop(0, blocks, push, 0)
+        lax.fori_loop(0, blocks, push, 0, unroll=4)
 
     prepare_own(table1)
     finish(lists)

time: 81.3 us -> 66.4 us (0.82)
  Pallas kernels: 75 us -> 60.1 us
    pallas_call x1, Pallas kernels: 75 us -> 60.1 us  [body(): pl.pallas_call(functools.partial(kernel, n_curve, n_group), out_shape=(tu...]
where the time goes in v2:
time: 66.4 us; the launch traced here: 66.1 us
  Pallas kernels  60.1 us (91%)
  local copies, waits for them, and re-layouts  5.32 us (8%)
  between operations  0.69 us (1%)
    pallas_call x1, Pallas kernels, body(): pl.pallas_call(functools.partial(kernel, n_curve, n_group), out_shape=(tu...  60.1 us
    unnamed x21, local copies, waits for them, and re-layouts  5.32 us

profile of v2, /device:TPU:0, one launch (start us, length us, event | category | flops | bytes accessed | tf_op | source)
XLA Modules:
  0.0 66.1 jit_solution(1357165566549287631)
XLA Ops:
  0.6 0.0 copy-start.4
  0.6 0.0 copy-start.3
  0.7 0.0 copy-start.5
  0.7 0.0 copy-start.6
  0.7 0.0 copy-start.7
  0.7 0.6 copy-done.4
  1.3 0.0 copy-done.3
  1.3 0.0 copy-done.5
  1.3 0.0 copy-done.6
  1.3 0.0 copy-done.7
  1.4 0.0 copy-start
  1.4 0.7 %copy-done = f32[1,16,3,128]{3,1,2,0:T(8,128)S(1)} copy-done((f32[1,16,3,128]{3,1,2,0:T(8,128)S(1)}, f32[1,16,3,128]{3,1,2,0:T(8,128)}, u32[]{:S(2)}) %copy-start) | copy-done | bytes 24600
  2.1 0.0 copy-start.1
  2.1 0.7 %copy-done.1 = f32[1,16,3,128]{3,1,2,0:T(8,128)S(1)} copy-done((f32[1,16,3,128]{3,1,2,0:T(8,128)S(1)}, f32[1,16,3,128]{3,1,2,0:T(8,128)}, u32[]{:S(2)}) %copy-start.1) | copy-done | bytes 24600
  2.8 0.0 copy-start.2
  2.8 0.7 %copy-done.2 = f32[1,16,128]{2,1,0:T(8,128)S(1)} copy-done((f32[1,16,128]{2,1,0:T(8,128)S(1)}, f32[1,16,128]{2,1,0:T(8,128)}, u32[]{:S(2)}) %copy-start.2) | copy-done | bytes 8216
  3.5 0.0 copy-start.8
  3.5 0.7 copy-done.8
  4.2 60.1 %sph.1 = (f32[1,3,16,128]{3,2,1,0:T(8,128)S(1)}, f32[1,3,16,128]{3,2,1,0:T(8,128)S(1)}, f32[1,16,128]{2,1,0:T(8,128)S(1)}) custom-call(f32[1,3,16,128]{3,2,1,0:T(8,128)S(1)} %bitcast.6, f32[1,3,16,128]{3,2,1,0:T(8,128)S(1)} %bitcast.7, f32[1,16,128]{2,1,0:T(8,128)S(1)} %copy-done.2, s32[1,16]{1,0:T(1,128)S(1)} %copy-done.6, s32[6,1,16]{2,1,0:T(1,128)S(1)} %bitcast.10, ...), custom_call_target="tpu_custom_call" | custom-call | tf_op jit(solution)/shard_map/sph/pallas_call | solution.py:385
  64.3 0.6 copy.15
  64.9 0.6 copy.16
  65.5 0.6 copy.17
Async XLA Ops:
  0.6 0.7 %copy-start.4 = (s32[1,16,6]{1,0,2:T(1,128)S(1)}, s32[1,16,6]{1,0,2:T(1,128)}, u32[]{:S(2)}) copy-start(s32[1,16,6]{1,0,2:T(1,128)} %param.16) | copy-start | bytes 1156
  0.6 0.7 %copy-start.3 = (s32[1,16,6]{1,0,2:T(1,128)S(1)}, s32[1,16,6]{1,0,2:T(1,128)}, u32[]{:S(2)}) copy-start(s32[1,16,6]{1,0,2:T(1,128)} %param.13) | copy-start | bytes 1156
  0.7 0.7 %copy-start.5 = (s32[1,16]{1,0:T(1,128)S(1)}, s32[1,16]{1,0:T(1,128)}, u32[]{:S(2)}) copy-start(s32[1,16]{1,0:T(1,128)} %slots_v.1) | copy-start | bytes 196
  0.7 0.7 %copy-start.6 = (s32[1,16]{1,0:T(1,128)S(1)}, s32[1,16]{1,0:T(1,128)}, u32[]{:S(2)}) copy-start(s32[1,16]{1,0:T(1,128)} %counts.1) | copy-start | bytes 196
  0.7 0.7 %copy-start.7 = (s32[1,8]{1,0:T(1,128)S(1)}, s32[1,8]{1,0:T(1,128)}, u32[]{:S(2)}) copy-start(s32[1,8]{1,0:T(1,128)} %sends1.1) | copy-start | bytes 100
  1.4 0.7 %copy-start = (f32[1,16,3,128]{3,1,2,0:T(8,128)S(1)}, f32[1,16,3,128]{3,1,2,0:T(8,128)}, u32[]{:S(2)}) copy-start(f32[1,16,3,128]{3,1,2,0:T(8,128)} %param.9) | copy-start | bytes 73732
  2.1 0.7 %copy-start.1 = (f32[1,16,3,128]{3,1,2,0:T(8,128)S(1)}, f32[1,16,3,128]{3,1,2,0:T(8,128)}, u32[]{:S(2)}) copy-start(f32[1,16,3,128]{3,1,2,0:T(8,128)} %param.10) | copy-start | bytes 73732
  2.8 0.7 %copy-start.2 = (f32[1,16,128]{2,1,0:T(8,128)S(1)}, f32[1,16,128]{2,1,0:T(8,128)}, u32[]{:S(2)}) copy-start(f32[1,16,128]{2,1,0:T(8,128)} %mass.1) | copy-start | bytes 24580
  3.5 0.7 copy-start.8

commit v3 on v2

--- a/solution.py
+++ b/solution.py
@@ -14,8 +14,7 @@
 TIME_STEP = 0.1
 SPACING = 0.6
 MOVE_CAP = 2
-LOG2E = math.log2(math.e)
-SCALE = -KERNEL_SCALE * LOG2E
+SCALE = -KERNEL_SCALE
 DEAD = -200.0
 MESH = pl.DeviceIdType.MESH
 F32 = jnp.float32
@@ -57,7 +56,7 @@
 def prepare_source(state, corner, source_t, source_m):
     row, state, after, square, cross = moments(state, corner)
     mass = state[6:7]
-    logm = jnp.where(mass > 0.0, jnp.log(jnp.maximum(mass, 1e-30)) * LOG2E, DEAD)
+    logm = jnp.where(mass > 0.0, jnp.log(jnp.maximum(mass, 1e-30)), DEAD)
     lower = jnp.where(row < 6, state, jnp.where(row == 6, 1.0, square))
     upper = jnp.where(row == 0, cross, jnp.where(row == 1, logm, 0.0))
     feature = jnp.concatenate([lower, upper], axis=0)
@@ -65,7 +64,7 @@
     pieces = source_rows(feature)
     used = len(pieces) * feature.shape[0]
     pieces.append(jnp.zeros((width - used, width), F32))
-    source_t[...] = jnp.concatenate(pieces, axis=0).T.astype(BF16)
+    source_t[...] = jnp.concatenate(pieces, axis=0).astype(BF16).T
     weighted = jnp.where(row < 7, lower * mass, 0.0)
     source_m[...] = jnp.concatenate(
         list(split(weighted)) + [jnp.zeros_like(weighted)], axis=0
@@ -99,34 +98,33 @@
     target_f[:, width : 2 * width] = table(closing, upper_c)
 
 
+def gather(block, nbr, table, axis):
+    picks = [block] + [nbr[item, 0, block] for item in range(nbr.shape[0])]
+    return picks, jnp.concatenate([table[pick] for pick in picks], axis=axis)
+
+
 def density_of(block, nbr, source_t, target_d):
-    count = nbr.shape[0]
     target = target_d[block]
-    total = None
-    for item in range(count + 1):
-        pick = block if item == 0 else nbr[item - 1, 0, block]
-        power = jnp.dot(source_t[pick], target, preferred_element_type=F32)
-        weight = jnp.exp2(power)
-        total = weight if total is None else total + weight
-    return BACKGROUND + jnp.sum(total, axis=0, keepdims=True)
+    _, sources = gather(block, nbr, source_t, 0)
+    weight = jnp.exp(jnp.dot(sources, target, preferred_element_type=F32))
+    return BACKGROUND + jnp.sum(weight, axis=0, keepdims=True)
 
 
 def force_of(block, nbr, state, corner, rho, rho_col, inv_col, source_t, source_m, target_f):
-    count = nbr.shape[0]
     width = state.shape[1]
-    target = target_f[block]
     inverse = 1.0 / rho
-    total = None
-    for item in range(count + 1):
-        pick = block if item == 0 else nbr[item - 1, 0, block]
-        both = jnp.dot(source_t[pick], target, preferred_element_type=F32)
-        soft = both[:, 0:width]
-        closing = jnp.maximum(both[:, width : 2 * width], 0.0)
+    picks, sources = gather(block, nbr, source_t, 0)
+    both = jnp.dot(sources, target_f[block], preferred_element_type=F32)
+    factors = []
+    for item, pick in enumerate(picks):
+        part = both[item * width : (item + 1) * width]
+        soft = part[:, 0:width]
+        closing = jnp.maximum(part[:, width : 2 * width], 0.0)
         bottom = soft * (rho_col[pick] + rho)
         viscous = closing * pl.reciprocal(bottom, approx=True)
-        factor = jnp.exp2(soft) * (inv_col[pick] + inverse - viscous)
-        part = jnp.dot(source_m[pick], factor.astype(BF16), preferred_element_type=F32)
-        total = part if total is None else total + part
+        factors.append((jnp.exp(soft) * (inv_col[pick] + inverse - viscous)).astype(BF16))
+    _, weighted = gather(block, nbr, source_m, 1)
+    total = jnp.dot(weighted, jnp.concatenate(factors, axis=0), preferred_element_type=F32)
     rows = state.shape[0]
     sums = total[0:rows] + total[rows : 2 * rows] + total[2 * rows : 3 * rows]
     row = rows_of(state.shape)
@@ -138,11 +136,15 @@
     return jnp.where(row < 3, position, jnp.where(row < 6, velocity, state))
 
 
-def columns(rho, rho_col, inv_col):
-    width = rho.shape[1]
-    col = jnp.broadcast_to(rho, (width, width)).T
-    rho_col[...] = col
-    inv_col[...] = 1.0 / col
+def columns(rho, start, rho_col, inv_col):
+    count, _, width = rho.shape
+    rows = jnp.concatenate([rho[item] for item in range(count)], axis=0)
+    turned = jnp.concatenate([rows, jnp.ones((width - count, width), F32)], axis=0).T
+    inverse = 1.0 / turned
+    for item in range(count):
+        shape = (width, width)
+        rho_col[start + item] = jnp.broadcast_to(turned[:, item : item + 1], shape)
+        inv_col[start + item] = jnp.broadcast_to(inverse[:, item : item + 1], shape)
 
 
 def kernel(
@@ -250,19 +252,13 @@
         copies = exchange(rho_send, rho, blocks, base)
 
         def own(block, carry):
-            value = density_of(block, nbr, source_t, target_d)
-            rho[block] = value
-            columns(value, rho_col.at[block], inv_col.at[block])
+            rho[block] = density_of(block, nbr, source_t, target_d)
             return carry
 
         lax.fori_loop(0, blocks, own, 0, unroll=4)
+        columns(rho.at[pl.ds(0, blocks)], 0, rho_col, inv_col)
         finish(copies)
-
-        def halos(block, carry):
-            columns(rho[block], rho_col.at[block], inv_col.at[block])
-            return carry
-
-        lax.fori_loop(blocks, blocks + 2 * halo, halos, 0, unroll=8)
+        columns(rho.at[pl.ds(blocks, 2 * halo)], blocks, rho_col, inv_col)
 
         def push(block, carry):
             write(
@@ -274,7 +270,7 @@
             )
             return carry
 
-        lax.fori_loop(0, blocks, push, 0, unroll=4)
+        lax.fori_loop(0, blocks, push, 0, unroll=2)
 
     prepare_own(table1)
     finish(lists)

time: 66.4 us -> 49.6 us (0.75)
  Pallas kernels: 60.1 us -> 43.2 us
    pallas_call x1, Pallas kernels: 60.1 us -> 43.2 us  [body(): pl.pallas_call(functools.partial(kernel, n_curve, n_group), out_shape=(tu...]
where the time goes in v3:
time: 49.6 us; the launch traced here: 49.2 us
  Pallas kernels  43.2 us (87%)
  local copies, waits for them, and re-layouts  5.32 us (11%)
  between operations  0.69 us (1%)
    pallas_call x1, Pallas kernels, body(): pl.pallas_call(functools.partial(kernel, n_curve, n_group), out_shape=(tu...  43.2 us
    unnamed x21, local copies, waits for them, and re-layouts  5.32 us

profile of v3, /device:TPU:0, one launch (start us, length us, event | category | flops | bytes accessed | tf_op | source)
XLA Modules:
  0.0 49.2 jit_solution(5193300441787506743)
XLA Ops:
  0.6 0.0 copy-start.4
  0.6 0.0 copy-start.3
  0.7 0.0 copy-start.5
  0.7 0.0 copy-start.6
  0.7 0.0 copy-start.7
  0.7 0.6 %copy-done.4 = s32[1,16,6]{1,0,2:T(1,128)S(1)} copy-done((s32[1,16,6]{1,0,2:T(1,128)S(1)}, s32[1,16,6]{1,0,2:T(1,128)}, u32[]{:S(2)}) %copy-start.4) | copy-done | bytes 408
  1.3 0.0 copy-done.3
  1.3 0.0 copy-done.5
  1.3 0.0 copy-done.6
  1.3 0.0 copy-done.7
  1.4 0.0 copy-start
  1.4 0.7 %copy-done = f32[1,16,3,128]{3,1,2,0:T(8,128)S(1)} copy-done((f32[1,16,3,128]{3,1,2,0:T(8,128)S(1)}, f32[1,16,3,128]{3,1,2,0:T(8,128)}, u32[]{:S(2)}) %copy-start) | copy-done | bytes 24600
  2.1 0.0 copy-start.1
  2.1 0.7 %copy-done.1 = f32[1,16,3,128]{3,1,2,0:T(8,128)S(1)} copy-done((f32[1,16,3,128]{3,1,2,0:T(8,128)S(1)}, f32[1,16,3,128]{3,1,2,0:T(8,128)}, u32[]{:S(2)}) %copy-start.1) | copy-done | bytes 24600
  2.8 0.0 copy-start.2
  2.8 0.7 %copy-done.2 = f32[1,16,128]{2,1,0:T(8,128)S(1)} copy-done((f32[1,16,128]{2,1,0:T(8,128)S(1)}, f32[1,16,128]{2,1,0:T(8,128)}, u32[]{:S(2)}) %copy-start.2) | copy-done | bytes 8216
  3.5 0.0 copy-start.8
  3.5 0.7 %copy-done.8 = s32[1,8]{1,0:T(1,128)S(1)} copy-done((s32[1,8]{1,0:T(1,128)S(1)}, s32[1,8]{1,0:T(1,128)}, u32[]{:S(2)}) %copy-start.8) | copy-done | bytes 56
  4.2 43.2 %sph.1 = (f32[1,3,16,128]{3,2,1,0:T(8,128)S(1)}, f32[1,3,16,128]{3,2,1,0:T(8,128)S(1)}, f32[1,16,128]{2,1,0:T(8,128)S(1)}) custom-call(f32[1,3,16,128]{3,2,1,0:T(8,128)S(1)} %bitcast.6, f32[1,3,16,128]{3,2,1,0:T(8,128)S(1)} %bitcast.7, f32[1,16,128]{2,1,0:T(8,128)S(1)} %copy-done.2, s32[1,16]{1,0:T(1,128)S(1)} %copy-done.6, s32[6,1,16]{2,1,0:T(1,128)S(1)} %bitcast.10, ...), custom_call_target="tpu_custom_call" | custom-call | tf_op jit(solution)/shard_map/sph/pallas_call | solution.py:381
  47.4 0.6 %copy.15 = f32[1,16,3,128]{3,1,2,0:T(8,128)} copy(f32[1,16,3,128]{3,1,2,0:T(8,128)S(1)} %bitcast.9) | data formatting | bytes 49152
  48.0 0.6 %copy.16 = f32[1,16,3,128]{3,1,2,0:T(8,128)} copy(f32[1,16,3,128]{3,1,2,0:T(8,128)S(1)} %bitcast.8) | data formatting | bytes 49152
  48.6 0.6 %copy.17 = f32[1,16,128]{2,1,0:T(8,128)} copy(f32[1,16,128]{2,1,0:T(8,128)S(1)} %get-tuple-element.14) | data formatting | bytes 16384
Async XLA Ops:
  0.6 0.7 %copy-start.4 = (s32[1,16,6]{1,0,2:T(1,128)S(1)}, s32[1,16,6]{1,0,2:T(1,128)}, u32[]{:S(2)}) copy-start(s32[1,16,6]{1,0,2:T(1,128)} %param.16) | copy-start | bytes 1156
  0.6 0.7 %copy-start.3 = (s32[1,16,6]{1,0,2:T(1,128)S(1)}, s32[1,16,6]{1,0,2:T(1,128)}, u32[]{:S(2)}) copy-start(s32[1,16,6]{1,0,2:T(1,128)} %param.13) | copy-start | bytes 1156
  0.7 0.7 %copy-start.5 = (s32[1,16]{1,0:T(1,128)S(1)}, s32[1,16]{1,0:T(1,128)}, u32[]{:S(2)}) copy-start(s32[1,16]{1,0:T(1,128)} %slots_v.1) | copy-start | bytes 196
  0.7 0.7 %copy-start.6 = (s32[1,16]{1,0:T(1,128)S(1)}, s32[1,16]{1,0:T(1,128)}, u32[]{:S(2)}) copy-start(s32[1,16]{1,0:T(1,128)} %counts.1) | copy-start | bytes 196
  0.7 0.7 %copy-start.7 = (s32[1,8]{1,0:T(1,128)S(1)}, s32[1,8]{1,0:T(1,128)}, u32[]{:S(2)}) copy-start(s32[1,8]{1,0:T(1,128)} %sends1.1) | copy-start | bytes 100
  1.4 0.7 %copy-start = (f32[1,16,3,128]{3,1,2,0:T(8,128)S(1)}, f32[1,16,3,128]{3,1,2,0:T(8,128)}, u32[]{:S(2)}) copy-start(f32[1,16,3,128]{3,1,2,0:T(8,128)} %param.9) | copy-start | bytes 73732
  2.1 0.7 %copy-start.1 = (f32[1,16,3,128]{3,1,2,0:T(8,128)S(1)}, f32[1,16,3,128]{3,1,2,0:T(8,128)}, u32[]{:S(2)}) copy-start(f32[1,16,3,128]{3,1,2,0:T(8,128)} %param.10) | copy-start | bytes 73732
  2.8 0.7 %copy-start.2 = (f32[1,16,128]{2,1,0:T(8,128)S(1)}, f32[1,16,128]{2,1,0:T(8,128)}, u32[]{:S(2)}) copy-start(f32[1,16,128]{2,1,0:T(8,128)} %mass.1) | copy-start | bytes 24580
  3.5 0.7 %copy-start.8 = (s32[1,8]{1,0:T(1,128)S(1)}, s32[1,8]{1,0:T(1,128)}, u32[]{:S(2)}) copy-start(s32[1,8]{1,0:T(1,128)} %sends2.1) | copy-start | bytes 100

commit v4 on v3

--- a/solution.py
+++ b/solution.py
@@ -15,7 +15,6 @@
 SPACING = 0.6
 MOVE_CAP = 2
 SCALE = -KERNEL_SCALE
-DEAD = -200.0
 MESH = pl.DeviceIdType.MESH
 F32 = jnp.float32
 BF16 = jnp.bfloat16
@@ -53,49 +52,52 @@
     return row, state, after, square, cross
 
 
-def prepare_source(state, corner, source_t, source_m):
+def prepare_source(state, corner, source_t):
     row, state, after, square, cross = moments(state, corner)
-    mass = state[6:7]
-    logm = jnp.where(mass > 0.0, jnp.log(jnp.maximum(mass, 1e-30)), DEAD)
     lower = jnp.where(row < 6, state, jnp.where(row == 6, 1.0, square))
-    upper = jnp.where(row == 0, cross, jnp.where(row == 1, logm, 0.0))
-    feature = jnp.concatenate([lower, upper], axis=0)
+    upper = jnp.where(row == 0, cross, 0.0)
+    pieces = source_rows(jnp.concatenate([lower, upper], axis=0))
     width = state.shape[1]
-    pieces = source_rows(feature)
-    used = len(pieces) * feature.shape[0]
+    used = len(pieces) * 2 * state.shape[0]
     pieces.append(jnp.zeros((width - used, width), F32))
     source_t[...] = jnp.concatenate(pieces, axis=0).astype(BF16).T
-    weighted = jnp.where(row < 7, lower * mass, 0.0)
-    source_m[...] = jnp.concatenate(
-        list(split(weighted)) + [jnp.zeros_like(weighted)], axis=0
-    ).astype(BF16)
-
-
-def prepare_target(state, corner, target_d, target_f):
+
+
+def prepare_target(state, corner, target):
     row, state, after, square, cross = moments(state, corner)
     width = state.shape[1]
     ahead = pltpu.roll(state, state.shape[0] - 3, 0)
-    near = jnp.where(row < 3, (-2.0 * SCALE) * state, 0.0)
-    tail = jnp.where(row == 7, SCALE, 0.0)
-    plain = jnp.where(row == 6, SCALE * square, near + tail)
-    soft = jnp.where(row == 6, SCALE * (square + SOFTENING), near + tail)
+    soft = jnp.where(
+        row < 3,
+        (-2.0 * SCALE) * state,
+        jnp.where(
+            row == 6, SCALE * (square + SOFTENING), jnp.where(row == 7, SCALE, 0.0)
+        ),
+    )
     closing = jnp.where(
         row < 3,
         -SCALE * ahead,
         jnp.where(row < 6, -SCALE * after, jnp.where(row == 6, SCALE * cross, 0.0)),
     )
-    upper_d = jnp.where(row == 1, 1.0, 0.0)
-    upper_c = jnp.where(row == 0, SCALE, 0.0)
-
-    def table(lower, upper):
-        pieces = target_rows(jnp.concatenate([lower, upper], axis=0))
-        used = len(pieces) * 2 * lower.shape[0]
+    upper = jnp.where(row == 0, SCALE, 0.0)
+
+    def table(low, high):
+        pieces = target_rows(jnp.concatenate([low, high], axis=0))
+        used = len(pieces) * 2 * low.shape[0]
         pieces.append(jnp.zeros((width - used, width), F32))
         return jnp.concatenate(pieces, axis=0).astype(BF16)
 
-    target_d[...] = table(plain, upper_d)
-    target_f[:, 0:width] = table(soft, jnp.zeros_like(upper_c))
-    target_f[:, width : 2 * width] = table(closing, upper_c)
+    target[:, 0:width] = table(soft, jnp.zeros_like(upper))
+    target[:, width : 2 * width] = table(closing, upper)
+
+
+def prepare_weights(state, corner, rho, source_m):
+    row = rows_of(state.shape)
+    mass = state[6:7]
+    centred = state - jnp.where(row == 0, corner + 0.5, jnp.where(row < 3, 0.5, 0.0))
+    weighted = jnp.where(row < 3, centred, jnp.where(row == 6, 1.0, 0.0)) * mass
+    both = jnp.concatenate([weighted, weighted * (1.0 / rho)], axis=0)
+    source_m[...] = jnp.concatenate(list(split(both)), axis=0).astype(BF16)
 
 
 def gather(block, nbr, table, axis):
@@ -103,48 +105,67 @@
     return picks, jnp.concatenate([table[pick] for pick in picks], axis=axis)
 
 
-def density_of(block, nbr, source_t, target_d):
-    target = target_d[block]
-    _, sources = gather(block, nbr, source_t, 0)
-    weight = jnp.exp(jnp.dot(sources, target, preferred_element_type=F32))
-    return BACKGROUND + jnp.sum(weight, axis=0, keepdims=True)
-
-
-def force_of(block, nbr, state, corner, rho, rho_col, inv_col, source_t, source_m, target_f):
+LIFT = math.exp(KERNEL_SCALE * SOFTENING)
+
+
+def listed_density(block, nbr, source_t, target, mass_col):
+    width = mass_col.shape[-1]
+    picks, sources = gather(block, nbr, source_t, 0)
+    soft = jnp.dot(sources, target[block][:, 0:width], preferred_element_type=F32)
+    total = None
+    for item, pick in enumerate(picks):
+        term = jnp.exp(soft[item * width : (item + 1) * width]) * mass_col[pick]
+        total = term if total is None else total + term
+    return BACKGROUND + LIFT * jnp.sum(total, axis=0, keepdims=True)
+
+
+def own_density(block, nbr, source_t, target, mass_col, weights, drags):
+    width = mass_col.shape[-1]
+    picks, sources = gather(block, nbr, source_t, 0)
+    both = jnp.dot(sources, target[block], preferred_element_type=F32)
+    total = None
+    for item, pick in enumerate(picks):
+        span = slice(item * width, (item + 1) * width)
+        soft = both[span, 0:width]
+        closing = jnp.maximum(both[span, width : 2 * width], 0.0)
+        weight = jnp.exp(soft)
+        term = weight * mass_col[pick]
+        total = term if total is None else total + term
+        weights[block, span, :] = weight.astype(BF16)
+        drags[block, span, :] = weight * (closing * pl.reciprocal(soft, approx=True))
+    return BACKGROUND + LIFT * jnp.sum(total, axis=0, keepdims=True)
+
+
+def force_of(block, nbr, state, corner, rho, rho_col, source_m, weights, drags):
     width = state.shape[1]
-    inverse = 1.0 / rho
-    picks, sources = gather(block, nbr, source_t, 0)
-    both = jnp.dot(sources, target_f[block], preferred_element_type=F32)
-    factors = []
+    picks, weighted = gather(block, nbr, source_m, 1)
+    parts = []
     for item, pick in enumerate(picks):
-        part = both[item * width : (item + 1) * width]
-        soft = part[:, 0:width]
-        closing = jnp.maximum(part[:, width : 2 * width], 0.0)
-        bottom = soft * (rho_col[pick] + rho)
-        viscous = closing * pl.reciprocal(bottom, approx=True)
-        factors.append((jnp.exp(soft) * (inv_col[pick] + inverse - viscous)).astype(BF16))
-    _, weighted = gather(block, nbr, source_m, 1)
-    total = jnp.dot(weighted, jnp.concatenate(factors, axis=0), preferred_element_type=F32)
+        drag = drags[block, item * width : (item + 1) * width, :]
+        parts.append((drag * pl.reciprocal(rho_col[pick] + rho, approx=True)).astype(BF16))
+    right = jnp.concatenate([weights[block], jnp.concatenate(parts, axis=0)], axis=1)
+    total = jnp.dot(weighted, right, preferred_element_type=F32)
     rows = state.shape[0]
-    sums = total[0:rows] + total[rows : 2 * rows] + total[2 * rows : 3 * rows]
+    total = total[0 : 2 * rows] + total[2 * rows : 4 * rows] + total[4 * rows : 6 * rows]
+    sums = (
+        total[0:rows, 0:width] * (1.0 / rho)
+        + total[rows : 2 * rows, 0:width]
+        - total[0:rows, width : 2 * width]
+    )
     row = rows_of(state.shape)
     centred = state - jnp.where(row == 0, corner + 0.5, jnp.where(row < 3, 0.5, 0.0))
-    strength = 2.0 * KERNEL_SCALE * math.exp(KERNEL_SCALE * SOFTENING)
-    accel = strength * (centred * sums[6:7] - sums)
+    accel = (2.0 * KERNEL_SCALE * LIFT) * (centred * sums[6:7] - sums)
     velocity = state + TIME_STEP * pltpu.roll(accel, 3, 0)
     position = state + TIME_STEP * pltpu.roll(velocity, rows - 3, 0)
     return jnp.where(row < 3, position, jnp.where(row < 6, velocity, state))
 
 
-def columns(rho, start, rho_col, inv_col):
-    count, _, width = rho.shape
-    rows = jnp.concatenate([rho[item] for item in range(count)], axis=0)
-    turned = jnp.concatenate([rows, jnp.ones((width - count, width), F32)], axis=0).T
-    inverse = 1.0 / turned
+def columns(rows, start, col):
+    count, width = len(rows), rows[0].shape[1]
+    rows = jnp.concatenate(rows, axis=0)
+    turned = jnp.concatenate([rows, jnp.zeros((width - count, width), F32)], axis=0).T
     for item in range(count):
-        shape = (width, width)
-        rho_col[start + item] = jnp.broadcast_to(turned[:, item : item + 1], shape)
-        inv_col[start + item] = jnp.broadcast_to(inverse[:, item : item + 1], shape)
+        col[start + item] = jnp.broadcast_to(turned[:, item : item + 1], (width, width))
 
 
 def kernel(
@@ -152,7 +173,7 @@
     pos, vel, mass, counts, nbr1, sends1, slots_s, slots_v, nbr2, sends2,
     pos_out, vel_out, rho_out,
     table1, table2, land1, land2, kept, moved, out1, out2, out_m, rho1, rho2, rho_s1, rho_s2,
-    source_t, source_m, target_d, target_f, rho_col, inv_col,
+    source_t, source_m, target, rho_col, mass_col, weights, drags,
     slots_own, slots_in, code_v, code_s,
     send_sem, recv_sem, send_g, recv_g, code_sem,
 ):
@@ -227,45 +248,60 @@
     def prepare_own(table):
         def run(block, carry):
             state = table[block]
-            prepare_source(state, corner, source_t.at[block], source_m.at[block])
-            prepare_target(state, corner, target_d.at[block], target_f.at[block])
+            prepare_source(state, corner, source_t.at[block])
+            prepare_target(state, corner, target.at[block])
             return carry
 
         lax.fori_loop(0, blocks, run, 0, unroll=8)
+        columns([table[block, 6:7, :] for block in range(blocks)], 0, mass_col)
 
     def prepare_halo(land):
         def run(item, carry):
-            block = blocks + item
-            prepare_source(land[item], corner, source_t.at[block], source_m.at[block])
+            prepare_source(land[item], corner, source_t.at[blocks + item])
             return carry
 
         lax.fori_loop(0, 2 * halo, run, 0, unroll=8)
+        columns([land[item, 6:7, :] for item in range(2 * halo)], blocks, mass_col)
 
     def sph(table, land, nbr, sends, rho, rho_send, base, write):
         prepare_halo(land)
 
         def listed(item, carry):
-            rho_send[item] = density_of(sends[0, item], nbr, source_t, target_d)
+            rho_send[item] = listed_density(sends[0, item], nbr, source_t, target, mass_col)
             return carry
 
         lax.fori_loop(0, 2 * halo, listed, 0, unroll=4)
         copies = exchange(rho_send, rho, blocks, base)
 
         def own(block, carry):
-            rho[block] = density_of(block, nbr, source_t, target_d)
-            return carry
-
-        lax.fori_loop(0, blocks, own, 0, unroll=4)
-        columns(rho.at[pl.ds(0, blocks)], 0, rho_col, inv_col)
+            rho[block] = own_density(
+                block, nbr, source_t, target, mass_col, weights, drags
+            )
+            return carry
+
+        lax.fori_loop(0, blocks, own, 0, unroll=2)
+        def weigh(block, carry):
+            prepare_weights(table[block], corner, rho[block], source_m.at[block])
+            return carry
+
+        lax.fori_loop(0, blocks, weigh, 0, unroll=4)
+        columns([rho[block] for block in range(blocks)], 0, rho_col)
         finish(copies)
-        columns(rho.at[pl.ds(blocks, 2 * halo)], blocks, rho_col, inv_col)
+        columns([rho[blocks + item] for item in range(2 * halo)], blocks, rho_col)
+
+        def weigh_halo(item, carry):
+            block = blocks + item
+            prepare_weights(land[item], corner, rho[block], source_m.at[block])
+            return carry
+
+        lax.fori_loop(0, 2 * halo, weigh_halo, 0, unroll=4)
 
         def push(block, carry):
             write(
                 block,
                 force_of(
                     block, nbr, table[block], corner, rho[block],
-                    rho_col, inv_col, source_t, source_m, target_f,
+                    rho_col, source_m, weights, drags,
                 ),
             )
             return carry
@@ -299,8 +335,8 @@
         one = jnp.int32(0)
         two = jnp.int32(0)
         for block in reversed(range(blocks)):
-            target = slots_s[0, block]
-            goes = (target >= other * blocks) & (target < (other + 1) * blocks)
+            owner = slots_s[0, block]
+            goes = (owner >= other * blocks) & (owner < (other + 1) * blocks)
             two = jnp.where(goes, one, two)
             one = jnp.where(goes, block, one)
         out_m[step, 0] = kept[one]
@@ -345,6 +381,7 @@
     halo = sends_first.shape[1] // 2
     whole = blocks + 2 * halo
     peers = n_group - 1
+    sources = neighbours_first.shape[2] + 1
     vmem = pl.BlockSpec(memory_space=pltpu.VMEM)
     smem = pl.BlockSpec(memory_space=pltpu.SMEM)
     scratch = [
@@ -362,11 +399,12 @@
         pltpu.VMEM((2 * halo, 1, width), F32),
         pltpu.VMEM((2 * halo, 1, width), F32),
         pltpu.VMEM((whole, width, width), BF16),
-        pltpu.VMEM((whole, 32, width), BF16),
-        pltpu.VMEM((blocks, width, width), BF16),
+        pltpu.VMEM((whole, 48, width), BF16),
         pltpu.VMEM((blocks, width, 2 * width), BF16),
         pltpu.VMEM((whole, width, width), F32),
         pltpu.VMEM((whole, width, width), F32),
+        pltpu.VMEM((blocks, sources * width, width), BF16),
+        pltpu.VMEM((blocks, sources * width, width), F32),
         pltpu.VMEM((1, width), jnp.int32),
         pltpu.VMEM((peers, 1, width), jnp.int32),
         pltpu.VMEM((blocks, width), jnp.int32),
@@ -389,7 +427,7 @@
         out_specs=(vmem, vmem, vmem),
         scratch_shapes=scratch,
         compiler_params=pltpu.CompilerParams(
-            collective_id=0, has_side_effects=True, vmem_limit_bytes=32 * 1024 * 1024
+            collective_id=0, has_side_effects=True, vmem_limit_bytes=56 * 1024 * 1024
         ),
         name="sph",
     )(

time: 49.6 us -> 38.8 us (0.78)
  Pallas kernels: 43.2 us -> 35.2 us
  local copies, waits for them, and re-layouts: 5.32 us -> 2.66 us
    pallas_call x1, Pallas kernels: 43.2 us -> 35.2 us  [body(): pl.pallas_call(functools.partial(kernel, n_curve, n_group), out_shape=(tu...]
    unnamed x21 -> x7, local copies, waits for them, and re-layouts: 5.32 us -> 2.66 us
where the time goes in v4:
time: 38.8 us; the launch traced here: 38.5 us
  Pallas kernels  35.2 us (91%)
  local copies, waits for them, and re-layouts  2.66 us (7%)
  between operations  0.65 us (2%)
    pallas_call x1, Pallas kernels, body(): pl.pallas_call(functools.partial(kernel, n_curve, n_group), out_shape=(tu...  35.2 us
    unnamed x7, local copies, waits for them, and re-layouts  2.66 us

profile of v4, /device:TPU:0, one launch (start us, length us, event | category | flops | bytes accessed | tf_op | source)
XLA Modules:
  0.0 38.5 jit_solution(14302772804682912989)
XLA Ops:
  0.6 35.2 %sph.1 = (f32[1,3,16,128]{3,2,1,0:T(8,128)}, f32[1,3,16,128]{3,2,1,0:T(8,128)}, f32[1,16,128]{2,1,0:T(8,128)}) custom-call(f32[1,3,16,128]{3,2,1,0:T(8,128)} %bitcast.6, f32[1,3,16,128]{3,2,1,0:T(8,128)} %bitcast.7, f32[1,16,128]{2,1,0:T(8,128)} %mass.1, s32[1,16]{1,0:T(1,128)} %counts.1, s32[6,1,16]{2,1,0:T(1,128)} %bitcast.10, s32[1,8]{1,0:T(1,128)} %sends1.1, ...), custom_call_target="tpu_custom_call" | custom-call | tf_op jit(solution)/shard_map/sph/pallas_call | solution.py:419
  35.9 0.0 copy-start
  35.9 1.4 %copy.15 = f32[1,16,3,128]{3,1,2,0:T(8,128)} copy(f32[1,16,3,128]{3,1,2,0:T(8,128)} %bitcast.9) | data formatting | bytes 49152
  37.2 0.0 copy-done
  37.2 0.0 copy-start.1
  37.2 0.6 %copy.16 = f32[1,16,3,128]{3,1,2,0:T(8,128)} copy(f32[1,16,3,128]{3,1,2,0:T(8,128)S(1)} %bitcast.8) | data formatting | bytes 49152
  37.8 0.1 copy-done.1
  37.9 0.6 %copy.17 = f32[1,16,128]{2,1,0:T(8,128)} copy(f32[1,16,128]{2,1,0:T(8,128)S(1)} %copy-done.1) | data formatting | bytes 16384
Async XLA Ops:
  35.9 1.4 %copy-start = (f32[1,3,16,128]{3,2,1,0:T(8,128)S(1)}, f32[1,3,16,128]{3,2,1,0:T(8,128)}, u32[]{:S(2)}) copy-start(f32[1,3,16,128]{3,2,1,0:T(8,128)} %get-tuple-element.7) | copy-start | bytes 73732
  37.2 0.7 %copy-start.1 = (f32[1,16,128]{2,1,0:T(8,128)S(1)}, f32[1,16,128]{2,1,0:T(8,128)}, u32[]{:S(2)}) copy-start(f32[1,16,128]{2,1,0:T(8,128)} %get-tuple-element.14) | copy-start | bytes 24580

commit v5 on v4

--- a/solution.py
+++ b/solution.py
@@ -100,18 +100,19 @@
     source_m[...] = jnp.concatenate(list(split(both)), axis=0).astype(BF16)
 
 
-def gather(block, nbr, table, axis):
+def gather(block, nbr, table, axis, place):
     picks = [block] + [nbr[item, 0, block] for item in range(nbr.shape[0])]
+    picks = [place(pick) for pick in picks]
     return picks, jnp.concatenate([table[pick] for pick in picks], axis=axis)
 
 
 LIFT = math.exp(KERNEL_SCALE * SOFTENING)
 
 
-def listed_density(block, nbr, source_t, target, mass_col):
+def listed_density(block, nbr, source_t, target, mass_col, place):
     width = mass_col.shape[-1]
-    picks, sources = gather(block, nbr, source_t, 0)
-    soft = jnp.dot(sources, target[block][:, 0:width], preferred_element_type=F32)
+    picks, sources = gather(block, nbr, source_t, 0, place)
+    soft = jnp.dot(sources, target[place(block), :, 0:width], preferred_element_type=F32)
     total = None
     for item, pick in enumerate(picks):
         term = jnp.exp(soft[item * width : (item + 1) * width]) * mass_col[pick]
@@ -119,10 +120,10 @@
     return BACKGROUND + LIFT * jnp.sum(total, axis=0, keepdims=True)
 
 
-def own_density(block, nbr, source_t, target, mass_col, weights, drags):
+def own_density(block, nbr, source_t, target, mass_col, weights, drags, place):
     width = mass_col.shape[-1]
-    picks, sources = gather(block, nbr, source_t, 0)
-    both = jnp.dot(sources, target[block], preferred_element_type=F32)
+    picks, sources = gather(block, nbr, source_t, 0, place)
+    both = jnp.dot(sources, target[place(block)], preferred_element_type=F32)
     total = None
     for item, pick in enumerate(picks):
         span = slice(item * width, (item + 1) * width)
@@ -138,7 +139,7 @@
 
 def force_of(block, nbr, state, corner, rho, rho_col, source_m, weights, drags):
     width = state.shape[1]
-    picks, weighted = gather(block, nbr, source_m, 1)
+    picks, weighted = gather(block, nbr, source_m, 1, lambda pick: pick)
     parts = []
     for item, pick in enumerate(picks):
         drag = drags[block, item * width : (item + 1) * width, :]
@@ -170,8 +171,9 @@
 
 def kernel(
     n_curve, n_group,
-    pos, vel, mass, counts, nbr1, sends1, slots_s, slots_v, nbr2, sends2,
+    pos_h, vel_h, mass_h, counts_h, nbr1_h, sends1_h, slots_h, nbr2_h, sends2_h,
     pos_out, vel_out, rho_out,
+    pos, vel, mass, counts, nbr1, sends1, slots_s, slots_v, nbr2, sends2, in_sem,
     table1, table2, land1, land2, kept, moved, out1, out2, out_m, rho1, rho2, rho_s1, rho_s2,
     source_t, source_m, target, rho_col, mass_col, weights, drags,
     slots_own, slots_in, code_v, code_s,
@@ -192,7 +194,21 @@
     for other in peers:
         pl.semaphore_signal(barrier, inc=1, device_id={"group": other}, device_id_type=MESH)
 
+    loads = [
+        pltpu.make_async_copy(source, landing, in_sem.at[item])
+        for item, (source, landing) in enumerate(
+            (
+                (pos_h, pos), (vel_h, vel), (mass_h, mass), (counts_h, counts),
+                (sends1_h, sends1), (slots_h, slots_v), (slots_h, slots_s),
+                (nbr1_h, nbr1), (nbr2_h, nbr2), (sends2_h, sends2),
+            )
+        )
+    ]
+    for load in loads:
+        load.start()
     lane = lax.broadcasted_iota(jnp.int32, (1, width), 1)
+    for load in loads:
+        load.wait()
 
     def load_state(block, carry):
         for axis in range(3):
@@ -245,29 +261,32 @@
         copy.start()
         lists.append(copy)
 
-    def prepare_own(table):
-        def run(block, carry):
-            state = table[block]
-            prepare_source(state, corner, source_t.at[block])
-            prepare_target(state, corner, target.at[block])
-            return carry
-
-        lax.fori_loop(0, blocks, run, 0, unroll=8)
-        columns([table[block, 6:7, :] for block in range(blocks)], 0, mass_col)
-
-    def prepare_halo(land):
+    def prepare(table, start, count, offset):
         def run(item, carry):
-            prepare_source(land[item], corner, source_t.at[blocks + item])
+            state = table[start + item]
+            prepare_source(state, corner, source_t.at[offset + item])
+            prepare_target(state, corner, target.at[offset + item])
+            return carry
+
+        lax.fori_loop(0, count, run, 0, unroll=8)
+        rows = [table[start + item, 6:7, :] for item in range(count)]
+        columns(rows, offset, mass_col)
+
+    def prepare_halo(land, offset):
+        def run(item, carry):
+            prepare_source(land[item], corner, source_t.at[offset + item])
             return carry
 
         lax.fori_loop(0, 2 * halo, run, 0, unroll=8)
-        columns([land[item, 6:7, :] for item in range(2 * halo)], blocks, mass_col)
-
-    def sph(table, land, nbr, sends, rho, rho_send, base, write):
-        prepare_halo(land)
+        columns([land[item, 6:7, :] for item in range(2 * halo)], offset, mass_col)
+
+    def sph(table, land, nbr, sends, rho, rho_send, base, offset, place, write):
+        prepare_halo(land, offset)
 
         def listed(item, carry):
-            rho_send[item] = listed_density(sends[0, item], nbr, source_t, target, mass_col)
+            rho_send[item] = listed_density(
+                sends[0, item], nbr, source_t, target, mass_col, place
+            )
             return carry
 
         lax.fori_loop(0, 2 * halo, listed, 0, unroll=4)
@@ -275,7 +294,7 @@
 
         def own(block, carry):
             rho[block] = own_density(
-                block, nbr, source_t, target, mass_col, weights, drags
+                block, nbr, source_t, target, mass_col, weights, drags, place
             )
             return carry
 
@@ -308,7 +327,7 @@
 
         lax.fori_loop(0, blocks, push, 0, unroll=2)
 
-    prepare_own(table1)
+    prepare(table1, 0, blocks, 0)
     finish(lists)
     wanted = rows_of((blocks, width)) + group * blocks
     lanes = lax.broadcasted_iota(jnp.int32, (blocks, width), 1)
@@ -320,7 +339,8 @@
         place = blocks + MOVE_CAP * step + jnp.where(lane > lead, 1, 0)
         code = code + jnp.sum(jnp.where(arrived == wanted, place, 0), axis=1, keepdims=True)
     code = jnp.minimum(code, moved.shape[0] - 1)
-    code_v[...] = jnp.broadcast_to(code, code_v.shape)
+    code_v[0:blocks, :] = jnp.broadcast_to(code, (blocks, width))
+    code_v[blocks:, :] = moved.shape[0] + rows_of((2 * halo, width))
     code_copy = pltpu.make_async_copy(code_v, code_s, code_sem)
     code_copy.start()
     finish(first)
@@ -328,8 +348,9 @@
     def keep(block, state):
         kept[block] = state
 
-    sph(table1, land1, nbr1, sends1, rho1, rho_s1, 2, keep)
-
+    sph(table1, land1, nbr1, sends1, rho1, rho_s1, 2, blocks, lambda pick: pick, keep)
+
+    moves_in = MOVE_CAP * (n_group - 1)
     moves = []
     for step, other in enumerate(peers):
         one = jnp.int32(0)
@@ -354,13 +375,14 @@
     code_copy.wait()
     for block in range(blocks):
         moved[block] = kept[block]
+    prepare(kept, 0, blocks, 0)
     finish(moves)
     for item in range(2 * halo):
         out2[item] = moved[code_s[sends2[0, item], 0]]
     second = exchange(out2, land2, 0, 4)
     for block in range(blocks):
         table2[block] = moved[code_s[block, 0]]
-    prepare_own(table2)
+    prepare(moved, blocks, moves_in, blocks)
     finish(second)
 
     def emit(block, state):
@@ -369,7 +391,10 @@
             vel_out[0, axis, pl.ds(block, 1), :] = state[3 + axis : 4 + axis]
         rho_out[0, pl.ds(block, 1), :] = rho2[block]
 
-    sph(table2, land2, nbr2, sends2, rho2, rho_s2, 6, emit)
+    sph(
+        table2, land2, nbr2, sends2, rho2, rho_s2, 6, blocks + moves_in,
+        lambda pick: code_s[pick, 0], emit,
+    )
 
 
 def body(
@@ -382,9 +407,22 @@
     whole = blocks + 2 * halo
     peers = n_group - 1
     sources = neighbours_first.shape[2] + 1
+    moves_in = MOVE_CAP * peers
     vmem = pl.BlockSpec(memory_space=pltpu.VMEM)
-    smem = pl.BlockSpec(memory_space=pltpu.SMEM)
-    scratch = [
+    places = [
+        pltpu.VMEM((1, 3, blocks, width), F32),
+        pltpu.VMEM((1, 3, blocks, width), F32),
+        pltpu.VMEM(masses.shape, F32),
+        pltpu.SMEM(counts.shape, jnp.int32),
+        pltpu.SMEM((sources - 1, 1, blocks), jnp.int32),
+        pltpu.SMEM(sends_first.shape, jnp.int32),
+        pltpu.SMEM(new_slot.shape, jnp.int32),
+        pltpu.VMEM(new_slot.shape, jnp.int32),
+        pltpu.SMEM((sources - 1, 1, blocks), jnp.int32),
+        pltpu.SMEM(sends_second.shape, jnp.int32),
+        pltpu.SemaphoreType.DMA((10,)),
+    ]
+    scratch = places + [
         pltpu.VMEM((blocks, 8, width), F32),
         pltpu.VMEM((blocks, 8, width), F32),
         pltpu.VMEM((2 * halo, 8, width), F32),
@@ -398,17 +436,17 @@
         pltpu.VMEM((whole, 1, width), F32),
         pltpu.VMEM((2 * halo, 1, width), F32),
         pltpu.VMEM((2 * halo, 1, width), F32),
-        pltpu.VMEM((whole, width, width), BF16),
+        pltpu.VMEM((whole + moves_in, width, width), BF16),
         pltpu.VMEM((whole, 48, width), BF16),
-        pltpu.VMEM((blocks, width, 2 * width), BF16),
+        pltpu.VMEM((blocks + moves_in, width, 2 * width), BF16),
         pltpu.VMEM((whole, width, width), F32),
-        pltpu.VMEM((whole, width, width), F32),
+        pltpu.VMEM((whole + moves_in, width, width), F32),
         pltpu.VMEM((blocks, sources * width, width), BF16),
         pltpu.VMEM((blocks, sources * width, width), F32),
         pltpu.VMEM((1, width), jnp.int32),
         pltpu.VMEM((peers, 1, width), jnp.int32),
-        pltpu.VMEM((blocks, width), jnp.int32),
-        pltpu.SMEM((blocks, width), jnp.int32),
+        pltpu.VMEM((whole, width), jnp.int32),
+        pltpu.SMEM((whole, width), jnp.int32),
         pltpu.SemaphoreType.DMA((8,)),
         pltpu.SemaphoreType.DMA((8,)),
         pltpu.SemaphoreType.DMA((2 * peers,)),
@@ -423,7 +461,7 @@
             turned,
             jax.ShapeDtypeStruct(masses.shape, F32),
         ),
-        in_specs=[vmem, vmem, vmem, smem, smem, smem, smem, vmem, smem, smem],
+        in_specs=[pl.BlockSpec(memory_space=pl.ANY)] * 9,
         out_specs=(vmem, vmem, vmem),
         scratch_shapes=scratch,
         compiler_params=pltpu.CompilerParams(
@@ -433,7 +471,7 @@
     )(
         positions.transpose(0, 2, 1, 3), velocities.transpose(0, 2, 1, 3), masses, counts,
         neighbours_first.transpose(2, 0, 1), sends_first, new_slot,
-        new_slot, neighbours_second.transpose(2, 0, 1), sends_second,
+        neighbours_second.transpose(2, 0, 1), sends_second,
     )
     return (
         positions_out.transpose(0, 2, 1, 3), velocities_out.transpose(0, 2, 1, 3), densities_out,

time: 38.8 us -> 38.1 us (0.982)
  Pallas kernels: 35.2 us -> 34.5 us
    pallas_call x1, Pallas kernels: 35.2 us -> 34.5 us  [body(): pl.pallas_call(functools.partial(kernel, n_curve, n_group), out_shape=(tu...]
where the time goes in v5:
time: 38.1 us; the launch traced here: 37.8 us
  Pallas kernels  34.5 us (91%)
  local copies, waits for them, and re-layouts  2.66 us (7%)
  between operations  0.65 us (2%)
    pallas_call x1, Pallas kernels, body(): pl.pallas_call(functools.partial(kernel, n_curve, n_group), out_shape=(tu...  34.5 us
    unnamed x7, local copies, waits for them, and re-layouts  2.66 us

profile of v5, /device:TPU:0, one launch (start us, length us, event | category | flops | bytes accessed | tf_op | source)
XLA Modules:
  0.0 37.8 jit_solution(5762595457479449686)
XLA Ops:
  0.6 34.5 %sph.1 = (f32[1,3,16,128]{3,2,1,0:T(8,128)}, f32[1,3,16,128]{3,2,1,0:T(8,128)}, f32[1,16,128]{2,1,0:T(8,128)}) custom-call(f32[1,3,16,128]{3,2,1,0:T(8,128)} %bitcast.8, f32[1,3,16,128]{3,2,1,0:T(8,128)} %bitcast.9, f32[1,16,128]{2,1,0:T(8,128)} %mass_h.1, s32[1,16]{1,0:T(1,128)} %counts_h.1, s32[6,1,16]{2,1,0:T(1,128)} %bitcast.10, s32[1,8]{1,0:T(1,128)} %sends1_h.1, ...), custom_call_target="tpu_custom_call" | custom-call | tf_op jit(solution)/shard_map/sph/pallas_call | solution.py:457
  35.1 0.0 copy-start
  35.1 1.4 %copy.15 = f32[1,16,3,128]{3,1,2,0:T(8,128)} copy(f32[1,16,3,128]{3,1,2,0:T(8,128)} %bitcast.7) | data formatting | bytes 49152
  36.5 0.0 copy-done
  36.5 0.0 copy-start.1
  36.5 0.6 %copy.16 = f32[1,16,3,128]{3,1,2,0:T(8,128)} copy(f32[1,16,3,128]{3,1,2,0:T(8,128)S(1)} %bitcast.6) | data formatting | bytes 49152
  37.1 0.1 copy-done.1
  37.2 0.6 %copy.17 = f32[1,16,128]{2,1,0:T(8,128)} copy(f32[1,16,128]{2,1,0:T(8,128)S(1)} %copy-done.1) | data formatting | bytes 16384
Async XLA Ops:
  35.1 1.4 %copy-start = (f32[1,3,16,128]{3,2,1,0:T(8,128)S(1)}, f32[1,3,16,128]{3,2,1,0:T(8,128)}, u32[]{:S(2)}) copy-start(f32[1,3,16,128]{3,2,1,0:T(8,128)} %get-tuple-element.7) | copy-start | bytes 73732
  36.5 0.7 %copy-start.1 = (f32[1,16,128]{2,1,0:T(8,128)S(1)}, f32[1,16,128]{2,1,0:T(8,128)}, u32[]{:S(2)}) copy-start(f32[1,16,128]{2,1,0:T(8,128)} %get-tuple-element.14) | copy-start | bytes 24580

commit v6 on v5

--- a/solution.py
+++ b/solution.py
@@ -14,6 +14,7 @@
 TIME_STEP = 0.1
 SPACING = 0.6
 MOVE_CAP = 2
+VMEM_BYTES = 56 * 1024 * 1024
 SCALE = -KERNEL_SCALE
 MESH = pl.DeviceIdType.MESH
 F32 = jnp.float32
@@ -107,17 +108,6 @@
 
 
 LIFT = math.exp(KERNEL_SCALE * SOFTENING)
-
-
-def listed_density(block, nbr, source_t, target, mass_col, place):
-    width = mass_col.shape[-1]
-    picks, sources = gather(block, nbr, source_t, 0, place)
-    soft = jnp.dot(sources, target[place(block), :, 0:width], preferred_element_type=F32)
-    total = None
-    for item, pick in enumerate(picks):
-        term = jnp.exp(soft[item * width : (item + 1) * width]) * mass_col[pick]
-        total = term if total is None else total + term
-    return BACKGROUND + LIFT * jnp.sum(total, axis=0, keepdims=True)
 
 
 def own_density(block, nbr, source_t, target, mass_col, weights, drags, place):
@@ -174,7 +164,7 @@
     pos_h, vel_h, mass_h, counts_h, nbr1_h, sends1_h, slots_h, nbr2_h, sends2_h,
     pos_out, vel_out, rho_out,
     pos, vel, mass, counts, nbr1, sends1, slots_s, slots_v, nbr2, sends2, in_sem,
-    table1, table2, land1, land2, kept, moved, out1, out2, out_m, rho1, rho2, rho_s1, rho_s2,
+    table1, table2, land1, land2, kept, moved, out1, out2, out_m, rho1, rho2, rho_i1, rho_i2, rho_s1, rho_s2,
     source_t, source_m, target, rho_col, mass_col, weights, drags,
     slots_own, slots_in, code_v, code_s,
     send_sem, recv_sem, send_g, recv_g, code_sem,
@@ -280,17 +270,8 @@
         lax.fori_loop(0, 2 * halo, run, 0, unroll=8)
         columns([land[item, 6:7, :] for item in range(2 * halo)], offset, mass_col)
 
-    def sph(table, land, nbr, sends, rho, rho_send, base, offset, place, write):
+    def sph(table, land, nbr, sends, rho, rho_in, rho_send, base, offset, place, write):
         prepare_halo(land, offset)
-
-        def listed(item, carry):
-            rho_send[item] = listed_density(
-                sends[0, item], nbr, source_t, target, mass_col, place
-            )
-            return carry
-
-        lax.fori_loop(0, 2 * halo, listed, 0, unroll=4)
-        copies = exchange(rho_send, rho, blocks, base)
 
         def own(block, carry):
             rho[block] = own_density(
@@ -299,6 +280,10 @@
             return carry
 
         lax.fori_loop(0, blocks, own, 0, unroll=2)
+        for item in range(2 * halo):
+            rho_send[item] = rho[sends[0, item]]
+        copies = exchange(rho_send, rho_in, 0, base)
+
         def weigh(block, carry):
             prepare_weights(table[block], corner, rho[block], source_m.at[block])
             return carry
@@ -306,11 +291,10 @@
         lax.fori_loop(0, blocks, weigh, 0, unroll=4)
         columns([rho[block] for block in range(blocks)], 0, rho_col)
         finish(copies)
-        columns([rho[blocks + item] for item in range(2 * halo)], blocks, rho_col)
+        columns([rho_in[item] for item in range(2 * halo)], blocks, rho_col)
 
         def weigh_halo(item, carry):
-            block = blocks + item
-            prepare_weights(land[item], corner, rho[block], source_m.at[block])
+            prepare_weights(land[item], corner, rho_in[item], source_m.at[blocks + item])
             return carry
 
         lax.fori_loop(0, 2 * halo, weigh_halo, 0, unroll=4)
@@ -348,7 +332,7 @@
     def keep(block, state):
         kept[block] = state
 
-    sph(table1, land1, nbr1, sends1, rho1, rho_s1, 2, blocks, lambda pick: pick, keep)
+    sph(table1, land1, nbr1, sends1, rho1, rho_i1, rho_s1, 2, blocks, lambda pick: pick, keep)
 
     moves_in = MOVE_CAP * (n_group - 1)
     moves = []
@@ -392,9 +376,21 @@
         rho_out[0, pl.ds(block, 1), :] = rho2[block]
 
     sph(
-        table2, land2, nbr2, sends2, rho2, rho_s2, 6, blocks + moves_in,
+        table2, land2, nbr2, sends2, rho2, rho_i2, rho_s2, 6, blocks + moves_in,
         lambda pick: code_s[pick, 0], emit,
     )
+
+
+def hand_over(first, second, third, first_out, second_out, third_out, sem):
+    pairs = ((first, first_out), (second, second_out), (third, third_out))
+    copies = [
+        pltpu.make_async_copy(source, landing, sem.at[item])
+        for item, (source, landing) in enumerate(pairs)
+    ]
+    for copy in copies:
+        copy.start()
+    for copy in copies:
+        copy.wait()
 
 
 def body(
@@ -432,8 +428,10 @@
         pltpu.VMEM((2 * halo, 8, width), F32),
         pltpu.VMEM((2 * halo, 8, width), F32),
         pltpu.VMEM((peers, MOVE_CAP, 8, width), F32),
-        pltpu.VMEM((whole, 1, width), F32),
-        pltpu.VMEM((whole, 1, width), F32),
+        pltpu.VMEM((blocks, 1, width), F32),
+        pltpu.VMEM((blocks, 1, width), F32),
+        pltpu.VMEM((2 * halo, 1, width), F32),
+        pltpu.VMEM((2 * halo, 1, width), F32),
         pltpu.VMEM((2 * halo, 1, width), F32),
         pltpu.VMEM((2 * halo, 1, width), F32),
         pltpu.VMEM((whole + moves_in, width, width), BF16),
@@ -465,7 +463,7 @@
         out_specs=(vmem, vmem, vmem),
         scratch_shapes=scratch,
         compiler_params=pltpu.CompilerParams(
-            collective_id=0, has_side_effects=True, vmem_limit_bytes=56 * 1024 * 1024
+            collective_id=0, has_side_effects=True, vmem_limit_bytes=VMEM_BYTES
         ),
         name="sph",
     )(
@@ -473,6 +471,17 @@
         neighbours_first.transpose(2, 0, 1), sends_first, new_slot,
         neighbours_second.transpose(2, 0, 1), sends_second,
     )
+    any_space = pl.BlockSpec(memory_space=pl.ANY)
+    shapes = (turned, turned, jax.ShapeDtypeStruct(masses.shape, F32))
+    positions_out, velocities_out, densities_out = pl.pallas_call(
+        hand_over,
+        out_shape=shapes,
+        in_specs=[any_space] * 3,
+        out_specs=(any_space,) * 3,
+        scratch_shapes=[pltpu.SemaphoreType.DMA((3,))],
+        compiler_params=pltpu.CompilerParams(vmem_limit_bytes=VMEM_BYTES),
+        name="hand_over",
+    )(positions_out, velocities_out, densities_out)
     return (
         positions_out.transpose(0, 2, 1, 3), velocities_out.transpose(0, 2, 1, 3), densities_out,
     )

time: 38.1 us -> 43.2 us (1.13)
  Pallas kernels: 34.5 us -> 42.3 us
  local copies, waits for them, and re-layouts: 2.66 us -> 0 us
    pallas_call x1, Pallas kernels: 34.5 us -> 39.5 us  [body(): pl.pallas_call(functools.partial(kernel, n_curve, n_group), out_shape=(tu...]
    pallas_call x0 -> x1, Pallas kernels: none -> 2.87 us  [body(): pl.pallas_call(hand_over, out_shape=shapes, in_specs=[any_space] * 3, out...]
    unnamed x7 -> x0, local copies, waits for them, and re-layouts: 2.66 us -> none
where the time goes in v6:
time: 43.2 us; the launch traced here: 43 us
  Pallas kernels  42.3 us (98%)
  between operations  0.64 us (1%)
    pallas_call x1, Pallas kernels, body(): pl.pallas_call(functools.partial(kernel, n_curve, n_group), out_shape=(tu...  39.5 us
    pallas_call x1, Pallas kernels, body(): pl.pallas_call(hand_over, out_shape=shapes, in_specs=[any_space] * 3, out...  2.87 us

profile of v6, /device:TPU:0, one launch (start us, length us, event | category | flops | bytes accessed | tf_op | source)
XLA Modules:
  0.0 43.0 jit_solution(8638045319759192523)
XLA Ops:
  0.6 39.5 %sph.1 = (f32[1,3,16,128]{3,2,1,0:T(8,128)}, f32[1,3,16,128]{3,2,1,0:T(8,128)}, f32[1,16,128]{2,1,0:T(8,128)}) custom-call(f32[1,3,16,128]{3,2,1,0:T(8,128)} %bitcast.6, f32[1,3,16,128]{3,2,1,0:T(8,128)} %bitcast.7, f32[1,16,128]{2,1,0:T(8,128)} %mass_h.1, s32[1,16]{1,0:T(1,128)} %counts_h.1, s32[6,1,16]{2,1,0:T(1,128)} %bitcast.8, s32[1,8]{1,0:T(1,128)} %sends1_h.1, ...), custom_call_target="tpu_custom_call" | custom-call | tf_op jit(solution)/shard_map/sph/pallas_call | solution.py:455
  40.1 2.9 %hand_over.1 = (f32[1,3,16,128]{3,2,1,0:T(8,128)}, f32[1,3,16,128]{3,2,1,0:T(8,128)}, f32[1,16,128]{2,1,0:T(8,128)}) custom-call(f32[1,3,16,128]{3,2,1,0:T(8,128)} %get-tuple-element.9.first, f32[1,3,16,128]{3,2,1,0:T(8,128)} %get-tuple-element.10.second, f32[1,16,128]{2,1,0:T(8,128)} %get-tuple-element.11.third), custom_call_target="tpu_custom_call" | custom-call | tf_op jit(solution)/shard_map/hand_over/pallas_call | solution.py:476

commit v7 on v5

--- a/solution.py
+++ b/solution.py
@@ -280,7 +280,7 @@
         lax.fori_loop(0, 2 * halo, run, 0, unroll=8)
         columns([land[item, 6:7, :] for item in range(2 * halo)], offset, mass_col)
 
-    def sph(table, land, nbr, sends, rho, rho_send, base, offset, place, write):
+    def sph(table, land, nbr, sends, rho, rho_send, base, offset, place, ahead, write):
         prepare_halo(land, offset)
 
         def listed(item, carry):
@@ -315,14 +315,16 @@
 
         lax.fori_loop(0, 2 * halo, weigh_halo, 0, unroll=4)
 
+        def pushed(block):
+            return force_of(
+                block, nbr, table[block], corner, rho[block],
+                rho_col, source_m, weights, drags,
+            )
+
+        ahead(pushed)
+
         def push(block, carry):
-            write(
-                block,
-                force_of(
-                    block, nbr, table[block], corner, rho[block],
-                    rho_col, source_m, weights, drags,
-                ),
-            )
+            write(block, pushed(block))
             return carry
 
         lax.fori_loop(0, blocks, push, 0, unroll=2)
@@ -348,40 +350,46 @@
     def keep(block, state):
         kept[block] = state
 
-    sph(table1, land1, nbr1, sends1, rho1, rho_s1, 2, blocks, lambda pick: pick, keep)
-
     moves_in = MOVE_CAP * (n_group - 1)
     moves = []
-    for step, other in enumerate(peers):
-        one = jnp.int32(0)
-        two = jnp.int32(0)
-        for block in reversed(range(blocks)):
-            owner = slots_s[0, block]
-            goes = (owner >= other * blocks) & (owner < (other + 1) * blocks)
-            two = jnp.where(goes, one, two)
-            one = jnp.where(goes, block, one)
-        out_m[step, 0] = kept[one]
-        out_m[step, 1] = kept[two]
-        copy = pltpu.make_async_remote_copy(
-            src_ref=out_m.at[step],
-            dst_ref=moved.at[pl.ds(blocks + MOVE_CAP * step, MOVE_CAP)],
-            send_sem=send_g.at[n_group - 1 + step],
-            recv_sem=recv_g.at[n_group - 1 + step],
-            device_id={"group": other},
-            device_id_type=MESH,
-        )
-        copy.start()
-        moves.append(copy)
+
+    def send_moving(pushed):
+        for step, other in enumerate(peers):
+            one = jnp.int32(0)
+            two = jnp.int32(0)
+            for block in reversed(range(blocks)):
+                owner = slots_s[0, block]
+                goes = (owner >= other * blocks) & (owner < (other + 1) * blocks)
+                two = jnp.where(goes, one, two)
+                one = jnp.where(goes, block, one)
+            out_m[step, 0] = pushed(one)
+            out_m[step, 1] = pushed(two)
+            copy = pltpu.make_async_remote_copy(
+                src_ref=out_m.at[step],
+                dst_ref=moved.at[pl.ds(blocks + MOVE_CAP * step, MOVE_CAP)],
+                send_sem=send_g.at[n_group - 1 + step],
+                recv_sem=recv_g.at[n_group - 1 + step],
+                device_id={"group": other},
+                device_id_type=MESH,
+            )
+            copy.start()
+            moves.append(copy)
+
+    sph(
+        table1, land1, nbr1, sends1, rho1, rho_s1, 2, blocks, lambda pick: pick,
+        send_moving, keep,
+    )
+
     code_copy.wait()
     for block in range(blocks):
         moved[block] = kept[block]
-    prepare(kept, 0, blocks, 0)
     finish(moves)
     for item in range(2 * halo):
         out2[item] = moved[code_s[sends2[0, item], 0]]
     second = exchange(out2, land2, 0, 4)
     for block in range(blocks):
         table2[block] = moved[code_s[block, 0]]
+    prepare(kept, 0, blocks, 0)
     prepare(moved, blocks, moves_in, blocks)
     finish(second)
 
@@ -393,7 +401,8 @@
 
     sph(
         table2, land2, nbr2, sends2, rho2, rho_s2, 6, blocks + moves_in,
-        lambda pick: code_s[pick, 0], emit,
+        lambda pick: code_s[pick, 0],
+        lambda pushed: None, emit,
     )
 
 

time: 38.1 us -> 36.3 us (0.953)
  Pallas kernels: 34.5 us -> 32.7 us
    pallas_call x1, Pallas kernels: 34.5 us -> 32.7 us  [body(): pl.pallas_call(functools.partial(kernel, n_curve, n_group), out_shape=(tu...]
where the time goes in v7:
time: 36.3 us; the launch traced here: 36 us
  Pallas kernels  32.7 us (90%)
  local copies, waits for them, and re-layouts  2.66 us (7%)
  between operations  0.65 us (2%)
    pallas_call x1, Pallas kernels, body(): pl.pallas_call(functools.partial(kernel, n_curve, n_group), out_shape=(tu...  32.7 us
    unnamed x7, local copies, waits for them, and re-layouts  2.66 us

profile of v7, /device:TPU:0, one launch (start us, length us, event | category | flops | bytes accessed | tf_op | source)
XLA Modules:
  0.0 36.0 jit_solution(2475373154466464477)
XLA Ops:
  0.6 32.7 %sph.1 = (f32[1,3,16,128]{3,2,1,0:T(8,128)}, f32[1,3,16,128]{3,2,1,0:T(8,128)}, f32[1,16,128]{2,1,0:T(8,128)}) custom-call(f32[1,3,16,128]{3,2,1,0:T(8,128)} %bitcast.8, f32[1,3,16,128]{3,2,1,0:T(8,128)} %bitcast.9, f32[1,16,128]{2,1,0:T(8,128)} %mass_h.1, s32[1,16]{1,0:T(1,128)} %counts_h.1, s32[6,1,16]{2,1,0:T(1,128)} %bitcast.10, s32[1,8]{1,0:T(1,128)} %sends1_h.1, ...), custom_call_target="tpu_custom_call" | custom-call | tf_op jit(solution)/shard_map/sph/pallas_call | solution.py:466
  33.3 0.0 copy-start
  33.3 1.4 %copy.15 = f32[1,16,3,128]{3,1,2,0:T(8,128)} copy(f32[1,16,3,128]{3,1,2,0:T(8,128)} %bitcast.7) | data formatting | bytes 49152
  34.7 0.0 copy-done
  34.7 0.0 copy-start.1
  34.7 0.6 %copy.16 = f32[1,16,3,128]{3,1,2,0:T(8,128)} copy(f32[1,16,3,128]{3,1,2,0:T(8,128)S(1)} %bitcast.6) | data formatting | bytes 49152
  35.3 0.1 copy-done.1
  35.4 0.6 %copy.17 = f32[1,16,128]{2,1,0:T(8,128)} copy(f32[1,16,128]{2,1,0:T(8,128)S(1)} %copy-done.1) | data formatting | bytes 16384
Async XLA Ops:
  33.3 1.4 %copy-start = (f32[1,3,16,128]{3,2,1,0:T(8,128)S(1)}, f32[1,3,16,128]{3,2,1,0:T(8,128)}, u32[]{:S(2)}) copy-start(f32[1,3,16,128]{3,2,1,0:T(8,128)} %get-tuple-element.7) | copy-start | bytes 73732
  34.7 0.7 %copy-start.1 = (f32[1,16,128]{2,1,0:T(8,128)S(1)}, f32[1,16,128]{2,1,0:T(8,128)}, u32[]{:S(2)}) copy-start(f32[1,16,128]{2,1,0:T(8,128)} %get-tuple-element.14) | copy-start | bytes 24580

commit v8 on v7

--- a/solution.py
+++ b/solution.py
@@ -289,7 +289,7 @@
             )
             return carry
 
-        lax.fori_loop(0, 2 * halo, listed, 0, unroll=4)
+        lax.fori_loop(0, 2 * halo, listed, 0, unroll=8)
         copies = exchange(rho_send, rho, blocks, base)
 
         def own(block, carry):
@@ -298,12 +298,12 @@
             )
             return carry
 
-        lax.fori_loop(0, blocks, own, 0, unroll=2)
+        lax.fori_loop(0, blocks, own, 0, unroll=4)
         def weigh(block, carry):
             prepare_weights(table[block], corner, rho[block], source_m.at[block])
             return carry
 
-        lax.fori_loop(0, blocks, weigh, 0, unroll=4)
+        lax.fori_loop(0, blocks, weigh, 0, unroll=8)
         columns([rho[block] for block in range(blocks)], 0, rho_col)
         finish(copies)
         columns([rho[blocks + item] for item in range(2 * halo)], blocks, rho_col)
@@ -313,7 +313,7 @@
             prepare_weights(land[item], corner, rho[block], source_m.at[block])
             return carry
 
-        lax.fori_loop(0, 2 * halo, weigh_halo, 0, unroll=4)
+        lax.fori_loop(0, 2 * halo, weigh_halo, 0, unroll=8)
 
         def pushed(block):
             return force_of(
@@ -327,7 +327,7 @@
             write(block, pushed(block))
             return carry
 
-        lax.fori_loop(0, blocks, push, 0, unroll=2)
+        lax.fori_loop(0, blocks, push, 0, unroll=8)
 
     prepare(table1, 0, blocks, 0)
     finish(lists)

time: 36.3 us -> 35.2 us (0.970)
  Pallas kernels: 32.7 us -> 31.6 us
    pallas_call x1, Pallas kernels: 32.7 us -> 31.6 us  [body(): pl.pallas_call(functools.partial(kernel, n_curve, n_group), out_shape=(tu...]
where the time goes in v8:
time: 35.2 us; the launch traced here: 34.9 us
  Pallas kernels  31.6 us (90%)
  local copies, waits for them, and re-layouts  2.66 us (8%)
  between operations  0.65 us (2%)
    pallas_call x1, Pallas kernels, body(): pl.pallas_call(functools.partial(kernel, n_curve, n_group), out_shape=(tu...  31.6 us
    unnamed x7, local copies, waits for them, and re-layouts  2.66 us

profile of v8, /device:TPU:0, one launch (start us, length us, event | category | flops | bytes accessed | tf_op | source)
XLA Modules:
  0.0 34.9 jit_solution(351131678366133970)
XLA Ops:
  0.6 31.6 %sph.1 = (f32[1,3,16,128]{3,2,1,0:T(8,128)}, f32[1,3,16,128]{3,2,1,0:T(8,128)}, f32[1,16,128]{2,1,0:T(8,128)}) custom-call(f32[1,3,16,128]{3,2,1,0:T(8,128)} %bitcast.8, f32[1,3,16,128]{3,2,1,0:T(8,128)} %bitcast.9, f32[1,16,128]{2,1,0:T(8,128)} %mass_h.1, s32[1,16]{1,0:T(1,128)} %counts_h.1, s32[6,1,16]{2,1,0:T(1,128)} %bitcast.10, s32[1,8]{1,0:T(1,128)} %sends1_h.1, ...), custom_call_target="tpu_custom_call" | custom-call | tf_op jit(solution)/shard_map/sph/pallas_call | solution.py:466
  32.2 0.0 copy-start
  32.2 1.4 %copy.15 = f32[1,16,3,128]{3,1,2,0:T(8,128)} copy(f32[1,16,3,128]{3,1,2,0:T(8,128)} %bitcast.7) | data formatting | bytes 49152
  33.6 0.0 copy-done
  33.6 0.0 copy-start.1
  33.6 0.6 %copy.16 = f32[1,16,3,128]{3,1,2,0:T(8,128)} copy(f32[1,16,3,128]{3,1,2,0:T(8,128)S(1)} %bitcast.6) | data formatting | bytes 49152
  34.2 0.1 copy-done.1
  34.3 0.6 %copy.17 = f32[1,16,128]{2,1,0:T(8,128)} copy(f32[1,16,128]{2,1,0:T(8,128)S(1)} %copy-done.1) | data formatting | bytes 16384
Async XLA Ops:
  32.2 1.4 %copy-start = (f32[1,3,16,128]{3,2,1,0:T(8,128)S(1)}, f32[1,3,16,128]{3,2,1,0:T(8,128)}, u32[]{:S(2)}) copy-start(f32[1,3,16,128]{3,2,1,0:T(8,128)} %get-tuple-element.7) | copy-start | bytes 73732
  33.6 0.7 %copy-start.1 = (f32[1,16,128]{2,1,0:T(8,128)S(1)}, f32[1,16,128]{2,1,0:T(8,128)}, u32[]{:S(2)}) copy-start(f32[1,16,128]{2,1,0:T(8,128)} %get-tuple-element.14) | copy-start | bytes 24580
